TPU v7x, 32 devices: a whole 2x2x4 slice. The times are simulated.
32 devices in a mesh: groups: 2 (over x), seq: 8 (over z, y), head: 2 (over core).
Axes of the slice: x: 2, y: 2, z: 4, core: 2. Of those that a mesh axis runs over, the one named last changes fastest.
Arguments:
- queries: bfloat16 [4096, 2048], P(('groups', 'seq'), 'head'), parts along dimension 0, may hold values from -24 to 24
- key_vectors: bfloat16 [4096, 2048], P(('groups', 'seq'), 'head'), parts along dimension 0, may hold values from -9 to 9
- value_vectors: bfloat16 [4096, 2048], P(('groups', 'seq'), 'head'), parts along dimension 0, may hold values from -6 to 6
- frozen_grad: bfloat16 [4096, 2048], P(('groups', 'seq'), 'head'), parts along dimension 0, may hold values from -6 to 6
- output_grad: bfloat16 [4096, 5376], P(('groups', 'seq'), 'head'), parts along dimension 0, may hold values from -6 to 6
- document_ids: int32 [4096], P('groups'), parts along dimension 0, may hold values from 0 to 7, never falling along the last dimension, each value on 1 to 768 neighbouring positions
- document_tenant: int32 [16], P('groups'), parts along dimension 0, may hold values from 0 to 7
- tenant_owner: int32 [8], replicated, may hold values from 0 to 7, each once
- phm_rule: float32 [16, 4, 4, 4], P('groups'), parts along dimension 0, may hold values from -3 to 3
- phm_left: float32 [16, 4, 512], P('groups'), parts along dimension 0, may hold values from -3 to 3
- phm_right: float32 [16, 4, 1344], P('groups'), parts along dimension 0, may hold values from -0.15625 to 0.15625
Outputs:
- query_grad: bfloat16 [4096, 2048], P(('groups', 'seq'), 'head'), parts along dimension 0
- key_grad: bfloat16 [4096, 2048], P(('groups', 'seq'), 'head'), parts along dimension 0
- value_grad: bfloat16 [4096, 2048], P(('groups', 'seq'), 'head'), parts along dimension 0
- rule_grad: float32 [16, 4, 4, 4], P(('groups', 'seq'), 'head'), parts along dimension 0
- left_grad: float32 [16, 4, 512], P(('groups', 'seq'), 'head'), parts along dimension 0
- right_grad: float32 [16, 4, 1344], P(('groups', 'seq'), 'head'), parts along dimension 0
There are 2 independent parts, one for each index of `groups`. A program takes and returns all parts, laid end to end along the dimension named above; an argument that names none is the same for every part. Nothing has to cross between parts.
Inputs may be any that keep to these rules, and one draw needn't show every extreme that they name: `document_ids`: never falling; each document holds 1 to 768 tokens, one exactly 768. `tenant_owner`: each seq index owns exactly one tenant.
All inputs are finite; a program needn't handle non-finite values.
Results may differ from a plain program's by a relative error of at most 0.009.
Values may be sent and summed in bfloat16 or wider, within the bound.
A program may use at most 128 MiB of HBM per device.

v0:
```python
import jax
import jax.numpy as jnp
from jax import lax
from jax.sharding import PartitionSpec as P

HEAD_DIM = 128
WINDOW = 512
PHM_N = 4


score_scale = 168.0 ** (-0.5)
neg_big = -1e30
highest = lax.Precision.HIGHEST


def passed_along(value, axis, steps):
    count = lax.axis_size(axis)
    first, last = (max(0, -steps), min(count, count - steps))
    return lax.ppermute(value, axis, [(source, source + steps) for source in range(first, last)])


def band_mask(query_pos, key_pos, query_docs, key_docs):
    later = query_pos[:, None] - key_pos[None, :]
    inside = (key_pos[None, :] >= 0) & (later >= 0) & (later < WINDOW)
    return inside & (query_docs[:, None] == key_docs[None, :])


def attend(query_part, key_part, value_part, cot_part, allowed):
    scores = (
        jnp.einsum("qgd,kgd->gqk", query_part, key_part, preferred_element_type=jnp.float32)
        * score_scale
    )
    scores = jnp.where(allowed[None], scores, neg_big)
    row_max = jnp.max(scores, axis=2, keepdims=True)
    expo_terms = jnp.exp(scores - row_max)
    attn_prob = expo_terms / jnp.sum(expo_terms, axis=2, keepdims=True)
    prob_low = attn_prob.astype(jnp.bfloat16)
    attn_out = jnp.einsum(
        "gqk,kgd->qgd", prob_low, value_part, preferred_element_type=jnp.float32
    ).astype(jnp.bfloat16)
    prob_grad = jnp.einsum("qgd,kgd->gqk", cot_part, value_part, preferred_element_type=jnp.float32)
    row_dot = jnp.sum(attn_prob * prob_grad, axis=2, keepdims=True)
    dscore = (attn_prob * (prob_grad - row_dot)).astype(jnp.bfloat16)
    query_term = (
        jnp.einsum("gqk,kgd->qgd", dscore, key_part, preferred_element_type=jnp.float32)
        * score_scale
    )
    key_term = (
        jnp.einsum("gqk,qgd->kgd", dscore, query_part, preferred_element_type=jnp.float32)
        * score_scale
    )
    value_term = jnp.einsum("gqk,qgd->kgd", prob_low, cot_part, preferred_element_type=jnp.float32)
    return (attn_out, query_term, key_term, value_term)


def on_device(
    queries,
    key_vectors,
    value_vectors,
    frozen_grad,
    output_grad,
    document_ids,
    document_tenant,
    tenant_owner,
    phm_rule,
    phm_left,
    phm_right,
):
    tok_rows = queries.shape[0]
    local_heads = queries.shape[1] // HEAD_DIM
    reach = (WINDOW + tok_rows - 2) // tok_rows
    seq_index = lax.axis_index("seq")
    head_index = lax.axis_index("head")
    head_count = lax.axis_size("head")
    tenants = tenant_owner.shape[0]
    block_count = PHM_N // head_count
    block_start = head_index * block_count
    head_shape = (tok_rows, local_heads, HEAD_DIM)
    query_heads = queries.reshape(head_shape)
    key_heads = key_vectors.reshape(head_shape)
    value_heads = value_vectors.reshape(head_shape)
    earlier = [
        passed_along((key_heads, value_heads), "seq", distance) for distance in range(reach, 0, -1)
    ]
    key_all = jnp.concatenate([received[0] for received in earlier] + [key_heads], axis=0)
    value_all = jnp.concatenate([received[1] for received in earlier] + [value_heads], axis=0)
    query_pos = seq_index * tok_rows + jnp.arange(tok_rows, dtype=jnp.int32)
    key_pos = (seq_index - reach) * tok_rows + jnp.arange((reach + 1) * tok_rows, dtype=jnp.int32)
    doc_lead = jnp.concatenate([jnp.zeros((reach * tok_rows,), jnp.int32), document_ids])
    key_docs = lax.dynamic_slice_in_dim(doc_lead, seq_index * tok_rows, (reach + 1) * tok_rows)
    query_docs = lax.dynamic_slice_in_dim(document_ids, seq_index * tok_rows, tok_rows)
    allowed = band_mask(query_pos, key_pos, query_docs, key_docs)
    tenant = document_tenant[query_docs]
    token_hot = (tenant[:, None] == jnp.arange(tenants, dtype=jnp.int32)[None, :]).astype(
        jnp.float32
    )
    rule_tok = phm_rule[tenant]
    left_tok = phm_left[tenant]
    right_tok = phm_right[tenant]
    cotangent = output_grad.astype(jnp.float32).reshape(
        tok_rows, block_count, sub_right_of(phm_right)
    )
    gate_here = jnp.einsum("tbq,tiq->tib", cotangent, right_tok, precision=highest)
    gate_terms = lax.all_gather(gate_here, "head", axis=2, tiled=True)
    rule_rows = lax.dynamic_slice_in_dim(rule_tok, block_start, block_count, 2)
    rule_mix = jnp.einsum("tiab,tib->tia", rule_rows, gate_terms, precision=highest)
    adapter = jnp.einsum("tia,tip->tap", rule_mix, left_tok, precision=highest)
    out_cot = (
        (frozen_grad.astype(jnp.float32) + adapter.reshape(tok_rows, -1))
        .astype(jnp.bfloat16)
        .reshape(head_shape)
    )
    group_size = min(2, local_heads)
    attn_parts, query_parts, key_parts, value_parts = ([], [], [], [])
    for head_start in range(0, local_heads, group_size):
        picked = slice(head_start, head_start + group_size)
        results = attend(
            query_heads[:, picked],
            key_all[:, picked],
            value_all[:, picked],
            out_cot[:, picked],
            allowed,
        )
        attn_parts.append(results[0])
        query_parts.append(results[1])
        key_parts.append(results[2])
        value_parts.append(results[3])
    attn_out = jnp.concatenate(attn_parts, axis=1)
    key_terms = jnp.concatenate(key_parts, axis=1)
    value_terms = jnp.concatenate(value_parts, axis=1)
    own_start = reach * tok_rows
    key_sum = key_terms[own_start:]
    value_sum = value_terms[own_start:]
    returned = [
        passed_along(
            (
                key_terms[(reach - distance) * tok_rows : (reach - distance + 1) * tok_rows],
                value_terms[(reach - distance) * tok_rows : (reach - distance + 1) * tok_rows],
            ),
            "seq",
            -distance,
        )
        for distance in range(1, reach + 1)
    ]
    for received in returned:
        key_sum = key_sum + received[0]
        value_sum = value_sum + received[1]
    query_grad = jnp.concatenate(query_parts, axis=1).reshape(tok_rows, -1).astype(jnp.bfloat16)
    key_grad = key_sum.reshape(tok_rows, -1).astype(jnp.bfloat16)
    value_grad = value_sum.reshape(tok_rows, -1).astype(jnp.bfloat16)
    left_in = attn_out.astype(jnp.float32).reshape(tok_rows, block_count, -1)
    left_here = jnp.einsum("tap,tip->tia", left_in, left_tok, precision=highest)
    left_proj = lax.all_gather(left_here, "head", axis=2, tiled=True)
    rule_cols = lax.dynamic_slice_in_dim(rule_tok, block_start, block_count, 3)
    rule_proj = jnp.einsum("tia,tiab->tib", left_proj, rule_cols, precision=highest)
    grad_scale = tok_rows ** (-0.5)
    rule_token = (left_here[:, :, :, None] * gate_terms[:, :, None, :]).reshape(tok_rows, -1)
    rule_local = grad_scale * jnp.einsum(
        "tx,tk->xk", token_hot, rule_token, precision=highest
    ).reshape(tenants, PHM_N, block_count, PHM_N)
    rule_part = lax.dynamic_update_slice_in_dim(
        jnp.zeros((tenants, PHM_N, PHM_N, PHM_N), jnp.float32), rule_local, block_start, 2
    )
    left_token = jnp.einsum("tia,tap->tip", rule_mix, left_in, precision=highest)
    left_part = grad_scale * jnp.einsum("tx,tip->xip", token_hot, left_token, precision=highest)
    right_token = jnp.einsum("tib,tbq->tiq", rule_proj, cotangent, precision=highest)
    right_part = grad_scale * jnp.einsum("tx,tiq->xiq", token_hot, right_token, precision=highest)
    owner_hot = (tenant_owner[:, None] == jnp.arange(tenants, dtype=jnp.int32)[None, :]).astype(
        jnp.float32
    )

    def to_owners(tenant_rows):
        moved = jnp.einsum("xo,x...->o...", owner_hot, tenant_rows, precision=highest)
        return moved.reshape((tenants, head_count, PHM_N // head_count) + tenant_rows.shape[2:])

    rule_owned = to_owners(rule_part)
    left_owned = to_owners(left_part)
    right_owned = to_owners(right_part)
    joined = (
        lax.psum_scatter(
            rule_owned.reshape((tenants * head_count,) + rule_owned.shape[2:]),
            ("seq", "head"),
            scatter_dimension=0,
            tiled=True,
        ),
        lax.psum_scatter(
            left_owned.reshape((tenants * head_count,) + left_owned.shape[2:]),
            ("seq", "head"),
            scatter_dimension=0,
            tiled=True,
        ),
        lax.psum_scatter(
            right_owned.reshape((tenants * head_count,) + right_owned.shape[2:]),
            ("seq", "head"),
            scatter_dimension=0,
            tiled=True,
        ),
    )
    rule_grad, left_grad, right_grad = joined
    return (query_grad, key_grad, value_grad, rule_grad, left_grad, right_grad)


def sub_right_of(phm_right):
    return phm_right.shape[2]


def solution(mesh):
    in_specs = (
        P(("groups", "seq"), "head"),
        P(("groups", "seq"), "head"),
        P(("groups", "seq"), "head"),
        P(("groups", "seq"), "head"),
        P(("groups", "seq"), "head"),
        P("groups"),
        P("groups"),
        P(),
        P("groups", None, None, None),
        P("groups", None, None),
        P("groups", None, None),
    )
    out_specs = (
        P(("groups", "seq"), "head"),
        P(("groups", "seq"), "head"),
        P(("groups", "seq"), "head"),
        P(("groups", "seq"), "head", None, None),
        P(("groups", "seq"), "head", None),
        P(("groups", "seq"), "head", None),
    )
    return jax.shard_map(
        on_device, mesh=mesh, in_specs=in_specs, out_specs=out_specs, check_vma=False
    )
```

profile of v0, /device:TPU:0, one launch (start us, length us, event | category | flops | bytes accessed | tf_op | source)
XLA Modules:
  0.0 310.6 jit_solution(9259128383112960532)
XLA Ops:
  7.2 1.3 copy.136
  9.6 5.7 %collective-permute-start.1 = (bf16[256,8,128]{2,0,1:T(8,128)(2,1)}, bf16[256,8,128]{2,0,1:T(8,128)(2,1)}, u32[]{:S(2)}, u32[]{:S(2)}) collective-permute-start(bf16[256,8,128]{2,0,1:T(8,128)(2,1)} %copy.137), channel_id=1, source_target_pairs={{0,2},{2,4},{4,6},{6,8},{8,10},{10,12},{12,14},{1,3},{3,5},{5,7},{... | collective-permute-start | bytes 1572872 | tf_op jit(solution)/shard_map/ppermute | solution.py:19
  15.2 3.5 %collective-permute-start = (bf16[256,8,128]{2,0,1:T(8,128)(2,1)}, bf16[256,8,128]{2,0,1:T(8,128)(2,1)}, u32[]{:S(2)}, u32[]{:S(2)}) collective-permute-start(bf16[256,8,128]{2,0,1:T(8,128)(2,1)} %copy.137), channel_id=1, source_target_pairs={{0,4},{2,6},{4,8},{6,10},{8,12},{10,14},{1,5},{3,7},{5,9},{7,11},{... | collective-permute-start | bytes 1572872 | tf_op jit(solution)/shard_map/ppermute | solution.py:19
  20.0 4.2 %collective-permute-start.3 = (bf16[256,8,128]{2,0,1:T(8,128)(2,1)}, bf16[256,8,128]{2,0,1:T(8,128)(2,1)}, u32[]{:S(2)}, u32[]{:S(2)}) collective-permute-start(bf16[256,8,128]{2,0,1:T(8,128)(2,1)} %copy.150), channel_id=1, source_target_pairs={{0,2},{2,4},{4,6},{6,8},{8,10},{10,12},{12,14},{1,3},{3,5},{5,7},{... | collective-permute-start | bytes 1572872 | tf_op jit(solution)/shard_map/ppermute | solution.py:19
  24.2 2.7 collective-permute-start.2
  27.8 5.2 %compare_select_fusion.2 = (s32[256]{0:T(256)S(1)}, s32[256]{0:T(256)S(1)}) fusion(s32[]{:T(128)} %bitcast.4, s32[]{:T(128)} %bitcast.5, s32[]{:T(128)} %bitcast.6, s32[]{:T(128)} %bitcast.7, s32[]{:T(128)} %bitcast.8, s32[]{:T(128)} %bitcast.9, s32[]{:T(128)} %bitcast.10, s32[]{:T(128)} %bitcast.11, s32[2048]{0:T(1024)S(1)} %copy-done.34, s32[]{:T(128)S(6)} %select_n.39), kind=kLoop, calls=%fused_computation.137 | loop fusion | flops 4352 | bytes 3108 | tf_op jit(solution)/shard_map/gather | solution.py:93
  33.0 1.9 gather_fusion
  34.8 6.2 %gather_fusion.1 = f32[256,4,1344]{2,1,0:T(4,128)} fusion(f32[8,4,1344]{2,1,0:T(4,128)S(1)} %copy-done, s32[1024]{0:T(1024)S(1)} %pad_clamp_fusion), kind=kCustom, calls=%fused_computation.1 | custom fusion | bytes 11011072 | tf_op jit(solution)/shard_map/gather | solution.py:99
  41.0 3.0 copy.144
  44.0 4.9 %copy.145 = bf16[256,2,1344]{2,1,0:T(2,128)(2,1)} copy(bf16[256,2,1344]{0,2,1:T(8,128)(2,1)} %bitcast.127) | data formatting | bytes 2752512 | tf_op jit(solution)/shard_map/reshape | solution.py:100
  48.9 15.3 %fusion.95 = f32[256,4,2]{1,2,0:T(2,128)S(1)} fusion(f32[256,4,1344]{2,1,0:T(4,128)} %gather_fusion.1, bf16[256,2,1344]{2,1,0:T(2,128)(2,1)} %copy.145), kind=kOutput, calls=%fused_computation.155 | convolution fusion | flops 33030144 | bytes 6889472 | tf_op jit(solution)/shard_map/tbq,tiq->tib/dot_general | solution.py:103
  64.4 1.8 all_gather.6
  66.4 3.1 gather_fusion.2
  69.6 1.6 multiply_reduce_fusion.5
  71.3 5.5 %fusion.96 = f32[256,2,512]{2,1,0:T(2,128)} fusion(f32[256,4,2]{2,1,0:T(4,128)S(1)} %multiply_reduce_fusion.5, f32[256,4,512]{2,1,0:T(4,128)S(1)} %copy-done.5), kind=kOutput, calls=%fused_computation.156 | convolution fusion | flops 12582912 | bytes 3153920 | tf_op jit(solution)/shard_map/tia,tip->tap/dot_general | solution.py:107
  77.8 2.3 copy.263
  80.1 1.2 copy.142
  82.7 2.1 fusion.43
  84.9 1.4 bitcast_select_fusion
  86.3 1.6 fusion.91
  87.9 1.4 bitcast_select_fusion.1
  89.4 1.7 fusion.92
  91.0 1.4 bitcast_select_fusion.2
  92.4 1.6 fusion.93
  94.0 1.4 bitcast_select_fusion.3
  95.5 1.5 fusion.94
  97.1 3.4 %convolution_bitcast_fusion = f32[768,2,128]{0,2,1:T(8,128)} fusion(bf16[256,8,128]{0,2,1:T(8,128)(2,1)S(1)} %bitcast.142, f32[2,256]{1,0:T(2,128)S(1)} %get-tuple-element.40, f32[2,256,768]{1,2,0:T(8,128)} %copy-done.20), kind=kOutput, calls=%fused_computation.37 | convolution fusion | flops 101844224 | bytes 2885632 | tf_op jit(solution)/shard_map/gqk,qgd->kgd/dot_general | solution.py:52
  100.5 3.3 %convolution_bitcast_fusion.1 = f32[768,2,128]{0,2,1:T(8,128)} fusion(bf16[256,8,128]{0,2,1:T(8,128)(2,1)S(1)} %bitcast.143, f32[2,256]{1,0:T(2,128)S(1)} %get-tuple-element.44, f32[2,256,768]{1,2,0:T(8,128)} %copy-done.21), kind=kOutput, calls=%fused_computation.38 | convolution fusion | flops 101844224 | bytes 2885632 | tf_op jit(solution)/shard_map/gqk,qgd->kgd/dot_general | solution.py:52
  103.9 3.3 %convolution_bitcast_fusion.2 = f32[768,2,128]{0,2,1:T(8,128)} fusion(bf16[256,8,128]{0,2,1:T(8,128)(2,1)S(1)} %bitcast.144, f32[2,256]{1,0:T(2,128)S(1)} %get-tuple-element.48, f32[2,256,768]{1,2,0:T(8,128)} %copy-done.22), kind=kOutput, calls=%fused_computation.39 | convolution fusion | flops 101844224 | bytes 2885632 | tf_op jit(solution)/shard_map/gqk,qgd->kgd/dot_general | solution.py:52
  107.2 3.4 %convolution_bitcast_fusion.3 = f32[768,2,128]{0,2,1:T(8,128)} fusion(bf16[256,8,128]{0,2,1:T(8,128)(2,1)S(1)} %bitcast.145, f32[2,256]{1,0:T(2,128)S(1)} %get-tuple-element.52, f32[2,256,768]{1,2,0:T(8,128)} %copy-done.23), kind=kOutput, calls=%fused_computation.40 | convolution fusion | flops 101844224 | bytes 2885632 | tf_op jit(solution)/shard_map/gqk,qgd->kgd/dot_general | solution.py:52
  110.6 2.7 fusion.30
  113.2 2.7 fusion.29
  115.9 3.3 %fusion.28 = bf16[256,2,128]{0,2,1:T(8,128)(2,1)} fusion(f32[2,256]{1,0:T(2,128)S(1)} %get-tuple-element.48, f32[2,256,768]{1,2,0:T(8,128)} %copy-done.22, bf16[256,8,128]{2,0,1:T(8,128)(2,1)} %copy.150, bf16[256,8,128]{2,0,1:T(8,128)(2,1)} %collective-permute-done.3, bf16[256,8,128]{2,0,1:T(8,128)(2,1)} %collective-permute-done.2), kind=kOutput, calls=%fused_computation.62 | convolution fusion | flops 106628352 | bytes 3278848 | tf_op jit(solution)/shard_map/gqk,kgd->qgd/dot_general | solution.py:38
  119.2 3.3 %fusion.27 = bf16[256,2,128]{0,2,1:T(8,128)(2,1)} fusion(f32[2,256]{1,0:T(2,128)S(1)} %get-tuple-element.52, f32[2,256,768]{1,2,0:T(8,128)} %copy-done.23, bf16[256,8,128]{2,0,1:T(8,128)(2,1)} %copy.150, bf16[256,8,128]{2,0,1:T(8,128)(2,1)} %collective-permute-done.3, bf16[256,8,128]{2,0,1:T(8,128)(2,1)} %collective-permute-done.2), kind=kOutput, calls=%fused_computation.61 | convolution fusion | flops 106628352 | bytes 3278848 | tf_op jit(solution)/shard_map/gqk,kgd->qgd/dot_general | solution.py:38
  122.6 1.0 pad_maximum_fusion.5
  123.6 1.4 copy.199
  125.0 4.9 %fusion.97 = f32[256,4,2]{1,2,0:T(2,128)S(1)} fusion(f32[256,4,512]{2,1,0:T(4,128)} %gather_fusion.2, bf16[256,2,512]{2,1,0:T(2,128)(2,1)} %copy.199), kind=kOutput, calls=%fused_computation.157 | convolution fusion | flops 12582912 | bytes 2629632 | tf_op jit(solution)/shard_map/tap,tip->tia/dot_general | solution.py:152
  129.9 3.2 %fusion.98 = f32[256,4,512]{2,1,0:T(4,128)} fusion(f32[256,4,2]{2,1,0:T(4,128)S(1)} %multiply_reduce_fusion.5, bf16[256,2,512]{2,1,0:T(2,128)(2,1)S(1)} %copy-done.17), kind=kOutput, calls=%fused_computation.158 | convolution fusion | flops 12582912 | bytes 2629632 | tf_op jit(solution)/shard_map/tia,tap->tip/dot_general | solution.py:164
  133.3 1.6 pad_maximum_fusion.3
  135.7 1.0 copy-done.8
  137.1 1.0 copy-done.7
  138.5 1.0 copy-done.6
  144.9 1.6 fusion.89
  147.5 1.4 collective-permute-start.5
  149.0 1.3 collective-permute-start.4
  150.5 1.7 fusion.88
  152.8 1.4 collective-permute-start.7
  154.2 1.3 collective-permute-start.6
  155.6 2.9 fusion.35
  159.4 1.8 all_gather.7
  161.2 1.0 copy.273
  162.2 4.1 %multiply_reduce_fusion = f32[256,4,2]{2,1,0:T(4,128)S(1)} fusion(f32[256,4,4,4]{3,2,1,0:T(4,128)S(1)} %gather_fusion, s32[]{:T(128)S(6)} %select_n.44, f32[256,4,4]{2,1,0:T(4,128)} %copy.273), kind=kLoop, calls=%fused_computation.12 | loop fusion | flops 14336 | bytes 57348 | tf_op jit(solution)/shard_map/tia,tiab->tib/dot_general | solution.py:155
  166.3 5.2 %fusion.99 = f32[256,4,1344]{2,1,0:T(4,128)S(1)} fusion(f32[256,4,2]{2,1,0:T(4,128)S(1)} %multiply_reduce_fusion, bf16[256,2,1344]{2,1,0:T(2,128)(2,1)S(1)} %copy-done.10), kind=kOutput, calls=%fused_computation.159 | convolution fusion | flops 33030144 | bytes 6889472 | tf_op jit(solution)/shard_map/tib,tbq->tiq/dot_general | solution.py:166
  171.5 2.0 fusion.6
  174.8 1.4 fusion.31
  176.2 1.4 fusion.32
  177.7 1.4 fusion.33
  179.1 1.4 fusion.34
  181.9 110.0 %all-reduce.1 = f32[16,2,4,4]{3,2,1,0:T(4,128)S(1)} all-reduce(f32[16,2,4,4]{3,2,1,0:T(4,128)S(1)} %bitcast.150), channel_id=2, replica_groups=mesh['groups'=2,'seq'=8,'head'=2] {'seq','head'}, use_global_device_ids=true, to_apply=%region_12.13.clone | all-reduce | flops 512 | bytes 4096
  291.9 1.3 constant_dynamic-slice_fusion.2
  293.2 2.0 constant_dynamic-slice_fusion.1
  295.2 2.0 constant_dynamic-slice_fusion
  297.2 2.0 fusion.42
  300.2 2.0 fusion.40
  (131 shorter events, 20.6 us)
Async XLA Ops:
  7.2 27.7 %copy-start = (f32[8,4,1344]{2,1,0:T(4,128)S(1)}, f32[8,4,1344]{2,1,0:T(4,128)}, u32[]{:S(2)}) copy-start(f32[8,4,1344]{2,1,0:T(4,128)} %param.21) | copy-start | bytes 516100
  7.2 11.6 %copy-start.28 = (bf16[256,1024]{1,0:T(8,128)(2,1)S(1)}, bf16[256,1024]{1,0:T(8,128)(2,1)}, u32[]{:S(2)}) copy-start(bf16[256,1024]{1,0:T(8,128)(2,1)} %param.13) | copy-start | bytes 1572868
  7.2 286.0 %all-reduce.7.cloned.1.call-start = ((), (), s32[]{:S(2)}) async-start(), calls=%async_computation | async-start | bytes 491520
  8.6 18.3 %copy-start.33 = (s32[8]{0:T(128)S(1)}, s32[8]{0:T(128)}, u32[]{:S(2)}) copy-start(s32[8]{0:T(128)} %param.17) | copy-start | bytes 100
  8.6 19.0 %copy-start.32 = (f32[8,4,4,4]{0,3,2,1:T(4,128)S(1)}, f32[8,4,4,4]{0,3,2,1:T(4,128)}, u32[]{:S(2)}) copy-start(f32[8,4,4,4]{0,3,2,1:T(4,128)} %param.19) | copy-start | bytes 6148
  8.6 19.2 %copy-start.34 = (s32[2048]{0:T(1024)S(1)}, s32[2048]{0:T(1024)}, u32[]{:S(2)}) copy-start(s32[2048]{0:T(1024)} %param.16) | copy-start | bytes 24580
  9.6 75.3 %collective-permute-start.1 = (bf16[256,8,128]{2,0,1:T(8,128)(2,1)}, bf16[256,8,128]{2,0,1:T(8,128)(2,1)}, u32[]{:S(2)}, u32[]{:S(2)}) collective-permute-start(bf16[256,8,128]{2,0,1:T(8,128)(2,1)} %copy.137), channel_id=1, source_target_pairs={{0,2},{2,4},{4,6},{6,8},{8,10},{10,12},{12,14},{1,3},{3,5},{5,7},{... | collective-permute-start | bytes 1572872 | tf_op jit(solution)/shard_map/ppermute | solution.py:19
  15.2 69.6 %collective-permute-start = (bf16[256,8,128]{2,0,1:T(8,128)(2,1)}, bf16[256,8,128]{2,0,1:T(8,128)(2,1)}, u32[]{:S(2)}, u32[]{:S(2)}) collective-permute-start(bf16[256,8,128]{2,0,1:T(8,128)(2,1)} %copy.137), channel_id=1, source_target_pairs={{0,4},{2,6},{4,8},{6,10},{8,12},{10,14},{1,5},{3,7},{5,9},{7,11},{... | collective-permute-start | bytes 1572872 | tf_op jit(solution)/shard_map/ppermute | solution.py:19
  20.0 90.6 %collective-permute-start.3 = (bf16[256,8,128]{2,0,1:T(8,128)(2,1)}, bf16[256,8,128]{2,0,1:T(8,128)(2,1)}, u32[]{:S(2)}, u32[]{:S(2)}) collective-permute-start(bf16[256,8,128]{2,0,1:T(8,128)(2,1)} %copy.150), channel_id=1, source_target_pairs={{0,2},{2,4},{4,6},{6,8},{8,10},{10,12},{12,14},{1,3},{3,5},{5,7},{... | collective-permute-start | bytes 1572872 | tf_op jit(solution)/shard_map/ppermute | solution.py:19
  24.2 86.4 %collective-permute-start.2 = (bf16[256,8,128]{2,0,1:T(8,128)(2,1)}, bf16[256,8,128]{2,0,1:T(8,128)(2,1)}, u32[]{:S(2)}, u32[]{:S(2)}) collective-permute-start(bf16[256,8,128]{2,0,1:T(8,128)(2,1)} %copy.150), channel_id=1, source_target_pairs={{0,4},{2,6},{4,8},{6,10},{8,12},{10,14},{1,5},{3,7},{5,9},{7,11},{... | collective-permute-start | bytes 1572872 | tf_op jit(solution)/shard_map/ppermute | solution.py:19
  64.2 2.2 copy-start.2
  69.6 1.6 copy-start.5
  71.2 5.6 %copy-start.29 = (bf16[256,1024]{1,0:T(8,128)(2,1)S(1)}, bf16[256,1024]{1,0:T(8,128)(2,1)}, u32[]{:S(2)}) copy-start(bf16[256,1024]{1,0:T(8,128)(2,1)} %param.11) | copy-start | bytes 1572868
  77.8 3.5 %copy-start.36 = (u32[32]{0:T(128)S(1)}, u32[32]{0:T(128)}, u32[]{:S(2)}) copy-start(u32[32]{0:T(128)} %constant.59) | copy-start | bytes 388
  81.3 3.5 %copy-start.18 = (bf16[256,1024]{0,1:T(8,128)(2,1)S(1)}, bf16[256,1024]{0,1:T(8,128)(2,1)}, u32[]{:S(2)}) copy-start(bf16[256,1024]{0,1:T(8,128)(2,1)} %copy.140) | copy-start | bytes 1572868
  86.3 1.6 copy-start.20
  89.3 1.7 copy-start.21
  92.4 1.6 copy-start.22
  95.4 1.7 copy-start.23
  95.5 1.7 copy-start.30
  125.0 4.9 %copy-start.17 = (bf16[256,2,512]{2,1,0:T(2,128)(2,1)S(1)}, bf16[256,2,512]{2,1,0:T(2,128)(2,1)}, u32[]{:S(2)}) copy-start(bf16[256,2,512]{2,1,0:T(2,128)(2,1)} %copy.199) | copy-start | bytes 1572868
  133.3 1.9 copy-start.9
  133.3 2.0 copy-start.31
  135.3 1.4 copy-start.8
  136.7 1.4 copy-start.7
  138.1 1.4 copy-start.6
  139.9 1.0 copy-start.19
  141.6 0.9 copy-start.11
  142.5 0.9 copy-start.13
  143.4 0.9 copy-start.15
  144.9 2.6 copy-start.3
  144.9 5.3 %copy-start.24 = (f32[768,2,128]{0,2,1:T(8,128)S(1)}, f32[768,2,128]{0,2,1:T(8,128)}, u32[]{:S(2)}) copy-start(f32[768,2,128]{0,2,1:T(8,128)} %convolution_bitcast_fusion) | copy-start | bytes 2359300
  144.9 5.3 %copy-start.25 = (f32[768,2,128]{0,2,1:T(8,128)S(1)}, f32[768,2,128]{0,2,1:T(8,128)}, u32[]{:S(2)}) copy-start(f32[768,2,128]{0,2,1:T(8,128)} %convolution_bitcast_fusion.1) | copy-start | bytes 2359300
  144.9 5.3 %copy-start.26 = (f32[768,2,128]{0,2,1:T(8,128)S(1)}, f32[768,2,128]{0,2,1:T(8,128)}, u32[]{:S(2)}) copy-start(f32[768,2,128]{0,2,1:T(8,128)} %convolution_bitcast_fusion.2) | copy-start | bytes 2359300
  144.9 5.3 %copy-start.27 = (f32[768,2,128]{0,2,1:T(8,128)S(1)}, f32[768,2,128]{0,2,1:T(8,128)}, u32[]{:S(2)}) copy-start(f32[768,2,128]{0,2,1:T(8,128)} %convolution_bitcast_fusion.3) | copy-start | bytes 2359300
  147.5 149.6 %collective-permute-start.5 = (f32[256,8,128]{0,2,1:T(8,128)}, f32[256,8,128]{0,2,1:T(8,128)}, u32[]{:S(2)}, u32[]{:S(2)}) collective-permute-start(f32[256,8,128]{0,2,1:T(8,128)} %get-tuple-element.31), channel_id=1, source_target_pairs={{4,0},{6,2},{8,4},{10,6},{12,8},{14,10},{5,1},{7,3},{9,5},{11,7},{... | collective-permute-start | bytes 3145736 | tf_op jit(solution)/shard_map/ppermute | solution.py:19
  149.0 148.2 %collective-permute-start.4 = (f32[256,8,128]{0,2,1:T(8,128)}, f32[256,8,128]{0,2,1:T(8,128)}, u32[]{:S(2)}, u32[]{:S(2)}) collective-permute-start(f32[256,8,128]{0,2,1:T(8,128)} %get-tuple-element.30), channel_id=1, source_target_pairs={{2,0},{4,2},{6,4},{8,6},{10,8},{12,10},{14,12},{3,1},{5,3},{7,5},{... | collective-permute-start | bytes 3145736 | tf_op jit(solution)/shard_map/ppermute | solution.py:19
  150.5 2.3 copy-start.4
  152.8 5.7 %copy-start.35 = (s32[8]{0:T(128)S(1)}, s32[8]{0:T(128)}, u32[]{:S(2)}) copy-start(s32[8]{0:T(128)} %param.18) | copy-start | bytes 100
  152.8 147.4 %collective-permute-start.7 = (f32[256,8,128]{0,2,1:T(8,128)}, f32[256,8,128]{0,2,1:T(8,128)}, u32[]{:S(2)}, u32[]{:S(2)}) collective-permute-start(f32[256,8,128]{0,2,1:T(8,128)} %get-tuple-element.29), channel_id=1, source_target_pairs={{4,0},{6,2},{8,4},{10,6},{12,8},{14,10},{5,1},{7,3},{9,5},{11,7},{... | collective-permute-start | bytes 3145736 | tf_op jit(solution)/shard_map/ppermute | solution.py:19
  154.2 146.0 %collective-permute-start.6 = (f32[256,8,128]{0,2,1:T(8,128)}, f32[256,8,128]{0,2,1:T(8,128)}, u32[]{:S(2)}, u32[]{:S(2)}) collective-permute-start(f32[256,8,128]{0,2,1:T(8,128)} %get-tuple-element.28), channel_id=1, source_target_pairs={{2,0},{4,2},{6,4},{8,6},{10,8},{12,10},{14,12},{3,1},{5,3},{7,5},{... | collective-permute-start | bytes 3145736 | tf_op jit(solution)/shard_map/ppermute | solution.py:19
  162.2 4.1 %copy-start.10 = (bf16[256,2,1344]{2,1,0:T(2,128)(2,1)S(1)}, bf16[256,2,1344]{2,1,0:T(2,128)(2,1)}, u32[]{:S(2)}) copy-start(bf16[256,2,1344]{2,1,0:T(2,128)(2,1)} %copy.145) | copy-start | bytes 4128772
  174.8 1.5 copy-start.12
  176.2 1.4 copy-start.14
  177.7 1.4 copy-start.16
  299.2 4.1 %copy-start.1 = (f32[8,4,1344]{2,1,0:T(4,128)S(1)}, f32[8,4,1344]{2,1,0:T(4,128)}, u32[]{:S(2)}) copy-start(f32[8,4,1344]{2,1,0:T(4,128)} %param.21) | copy-start | bytes 516100
Sparse Core Ops, SparseCore 0:
  174.9 98.3 all-reduce.6
where the time goes:
time: 316 us; the launch traced here: 311 us
  blocking collectives  114 us (36%)
  matrix products  79.3 us (25%)
  local copies, waits for them, and re-layouts  52.3 us (17%)
  other arithmetic  28.6 us (9%)
  starting transfers between devices  21.5 us (7%)
  between operations  15.2 us (5%)
    unnamed x1, blocking collectives  110 us
    unnamed x89, local copies, waits for them, and re-layouts  24.4 us
    ppermute x8, starting transfers between devices, passed_along(): lax.ppermute(value, axis, [(source, source + steps) for source in range(f...  21.5 us
    dot_general x1, matrix products, on_device(): jnp.einsum('tbq,tiq->tib', cotangent, right_tok, precision=highest)  15.3 us
    dot_general x4, matrix products, attend(): jnp.einsum('gqk,qgd->kgd', prob_low, cot_part, preferred_element_type=jnp...  13.5 us
    dot_general x4, matrix products, attend(): jnp.einsum('gqk,kgd->qgd', prob_low, value_part, preferred_element_type=j...  12 us
    sub x4, other arithmetic, attend(): expo_terms = jnp.exp(scores - row_max)  6.43 us
  transfers between devices with their start and end apart: 9, of which 0 were waited for; matrix products, arithmetic and copies ran while one was open for 38% of the time, Pallas kernels for 0%

commit v1 on v0

v1 whole, which is shorter than its diff:
```python
import functools

import jax
import jax.numpy as jnp
from jax import lax
from jax.experimental import pallas as pl
from jax.experimental.pallas import tpu as pltpu
from jax.sharding import PartitionSpec as P

HEAD_DIM = 128
WINDOW = 512
PHM_N = 4
MESH = pl.DeviceIdType.MESH

score_scale = 168.0 ** (-0.5)
neg_big = -1e30
f32 = jnp.float32
bf16 = jnp.bfloat16


def passed_along(value, axis, steps):
    count = lax.axis_size(axis)
    first, last = (max(0, -steps), min(count, count - steps))
    return lax.ppermute(value, axis, [(source, source + steps) for source in range(first, last)])


def split_two(value):
    high = lax.reduce_precision(value, 8, 7)
    return high.astype(bf16), (value - high).astype(bf16)


def kernel_split(value):
    high = value.astype(bf16)
    return high, (value - high.astype(f32)).astype(bf16)


def dot_nt(a, b):
    return lax.dot_general(a, b, (((1,), (1,)), ((), ())), preferred_element_type=f32)


def dot_nn(a, b):
    return lax.dot_general(a, b, (((1,), (0,)), ((), ())), preferred_element_type=f32)


def dot_tn(a, b):
    return lax.dot_general(a, b, (((0,), (0,)), ((), ())), preferred_element_type=f32)


def attention_kernel(reach, heads_per_block, *refs):
    blocks = reach + 1
    q_ref, frozen_ref = refs[0:2]
    k_refs = refs[2 : 2 + blocks]
    v_refs = refs[2 + blocks : 2 + 2 * blocks]
    gate_ref, qinfo_ref, kdoc_ref, rule_ref, lhi_ref, llo_ref = refs[2 + 2 * blocks : 8 + 2 * blocks]
    dq_ref, own_ref = refs[8 + 2 * blocks : 10 + 2 * blocks]
    back_refs = refs[10 + 2 * blocks : 10 + 2 * blocks + reach]
    proj_ref, left_ref, bias_ref = refs[10 + 2 * blocks + reach :]
    rows = q_ref.shape[0]
    head = pl.program_id(0)
    block = head // heads_per_block
    part = lax.rem(head, heads_per_block)

    @pl.when(head == 0)
    def _():
        query_pos = lax.broadcasted_iota(jnp.int32, (rows, rows), 0)
        key_pos = lax.broadcasted_iota(jnp.int32, (rows, rows), 1)
        for j in range(blocks):
            later = query_pos - key_pos + (reach - j) * rows
            same = qinfo_ref[:, 0:1] == kdoc_ref[:, j * rows : (j + 1) * rows]
            allowed = same & (later >= 0) & (later < WINDOW)
            bias_ref[:, j * rows : (j + 1) * rows] = jnp.where(allowed, 0.0, neg_big)

    mix = jnp.zeros(gate_ref.shape[1:], f32)
    for b in range(PHM_N):
        mix = mix + gate_ref[b] * rule_ref[block, b : b + 1, :]
    mix_hi, mix_lo = kernel_split(mix)
    columns = pl.ds(pl.multiple_of(part * HEAD_DIM, HEAD_DIM), HEAD_DIM)
    lhi = lhi_ref[:, columns]
    llo = llo_ref[:, columns]
    adapter = dot_nn(mix_hi, lhi) + dot_nn(mix_lo, lhi) + dot_nn(mix_hi, llo)
    cot = (frozen_ref[...].astype(f32) + adapter).astype(bf16)
    q = q_ref[...]
    scores = [
        dot_nt(q, k_refs[j][...]) * score_scale + bias_ref[:, j * rows : (j + 1) * rows]
        for j in range(blocks)
    ]
    row_max = functools.reduce(jnp.maximum, [jnp.max(s, axis=1, keepdims=True) for s in scores])
    expo = [jnp.exp(s - row_max) for s in scores]
    total = functools.reduce(jnp.add, [jnp.sum(e, axis=1, keepdims=True) for e in expo])
    inverse = 1.0 / total
    prob = [e * inverse for e in expo]
    low = [p.astype(bf16) for p in prob]
    out = functools.reduce(jnp.add, [dot_nn(low[j], v_refs[j][...]) for j in range(blocks)])
    out = out.astype(bf16)
    grad = [dot_nt(cot, v_refs[j][...]) for j in range(blocks)]
    row_dot = functools.reduce(
        jnp.add, [jnp.sum(prob[j] * grad[j], axis=1, keepdims=True) for j in range(blocks)]
    )
    dscore = [(prob[j] * (grad[j] - row_dot)).astype(bf16) for j in range(blocks)]
    dq = functools.reduce(jnp.add, [dot_nn(dscore[j], k_refs[j][...]) for j in range(blocks)])
    dq_ref[...] = (dq * score_scale).astype(bf16)
    for j in range(blocks):
        target = own_ref if j == reach else back_refs[j]
        target[0] = (dot_tn(dscore[j], q) * score_scale).astype(target.dtype)
        target[1] = dot_tn(low[j], cot).astype(target.dtype)
    width = proj_ref.shape[2]
    slot = lax.broadcasted_iota(jnp.int32, (rows, width), 1) // PHM_N
    proj = jnp.where(slot == qinfo_ref[:, 1:2], dot_nt(out, lhi) + dot_nt(out, llo), 0.0)
    left = dot_tn(mix_hi, out) + dot_tn(mix_lo, out)

    @pl.when(part == 0)
    def _():
        proj_ref[0] = proj

    @pl.when(part != 0)
    def _():
        proj_ref[0] += proj

    @pl.when(block == 0)
    def _():
        left_ref[:, columns] = left

    @pl.when(block != 0)
    def _():
        left_ref[:, columns] += left


def attention(queries, frozen, keys, values, gate, qinfo, kdoc, rule, lhi, llo, block_count):
    rows, width = queries.shape
    local_heads = width // HEAD_DIM
    reach = len(keys) - 1
    heads_per_block = local_heads // block_count
    factor_columns = gate.shape[2]

    def per_head():
        return pl.BlockSpec((rows, HEAD_DIM), lambda h: (0, h))

    def pair():
        return pl.BlockSpec((2, rows, HEAD_DIM), lambda h: (0, 0, h))

    def whole(array):
        return pl.BlockSpec(array.shape, lambda h: (0,) * array.ndim)

    left_shape = jax.ShapeDtypeStruct(lhi.shape, f32)
    return pl.pallas_call(
        functools.partial(attention_kernel, reach, heads_per_block),
        grid=(local_heads,),
        in_specs=[per_head() for _ in range(2 + 2 * (reach + 1))]
        + [whole(a) for a in (gate, qinfo, kdoc, rule, lhi, llo)],
        out_specs=[per_head(), pair()]
        + [pair() for _ in range(reach)]
        + [
            pl.BlockSpec((1, rows, factor_columns), lambda h: (h // heads_per_block, 0, 0)),
            whole(left_shape),
        ],
        out_shape=[
            jax.ShapeDtypeStruct((rows, width), bf16),
            jax.ShapeDtypeStruct((2, rows, width), f32),
        ]
        + [jax.ShapeDtypeStruct((2, rows, width), bf16) for _ in range(reach)]
        + [jax.ShapeDtypeStruct((block_count, rows, factor_columns), f32), left_shape],
        scratch_shapes=[pltpu.VMEM((rows, (reach + 1) * rows), f32)],
        compiler_params=pltpu.CompilerParams(vmem_limit_bytes=32 * 2**20),
        cost_estimate=pl.CostEstimate(
            flops=12 * rows * rows * (reach + 1) * width,
            bytes_accessed=40 * rows * width,
            transcendentals=rows * rows * (reach + 1) * local_heads,
        ),
    )(queries, frozen, *keys, *values, gate, qinfo, kdoc, rule, lhi, llo)


def exchange_kernel(seq_count, head_count, x_ref, o_ref, landed, send_sem, recv_sem):
    count = seq_count * head_count
    me = lax.axis_index("seq") * head_count + lax.axis_index("head")

    def device(step):
        peer = lax.rem(me + step, count)
        return peer, {"seq": peer // head_count, "head": lax.rem(peer, head_count)}

    barrier = pltpu.get_barrier_semaphore()
    for step in range(1, count):
        pl.semaphore_signal(barrier, inc=1, device_id=device(step)[1], device_id_type=MESH)
    pl.semaphore_wait(barrier, count - 1)
    copies = []
    for step in range(1, count):
        peer, where = device(step)
        copy = pltpu.make_async_remote_copy(
            src_ref=x_ref.at[peer],
            dst_ref=landed.at[step],
            send_sem=send_sem.at[step],
            recv_sem=recv_sem.at[step],
            device_id=where,
            device_id_type=MESH,
        )
        copy.start()
        copies.append(copy)
    total = x_ref[me]
    for step in range(1, count):
        copies[step - 1].wait_recv()
        total = total + landed[step]
    o_ref[...] = total
    for copy in copies:
        copy.wait_send()


def exchange_sum(pieces, seq_count, head_count):
    count = seq_count * head_count
    return pl.pallas_call(
        functools.partial(exchange_kernel, seq_count, head_count),
        out_shape=jax.ShapeDtypeStruct(pieces.shape[1:], f32),
        in_specs=[pl.BlockSpec(memory_space=pltpu.VMEM)],
        out_specs=pl.BlockSpec(memory_space=pltpu.VMEM),
        scratch_shapes=[
            pltpu.VMEM(pieces.shape, f32),
            pltpu.SemaphoreType.DMA((count,)),
            pltpu.SemaphoreType.DMA((count,)),
        ],
        compiler_params=pltpu.CompilerParams(
            collective_id=0, has_side_effects=True, vmem_limit_bytes=32 * 2**20
        ),
        cost_estimate=pl.CostEstimate(
            flops=pieces.size, bytes_accessed=8 * pieces.size, transcendentals=0
        ),
    )(pieces)


def on_device(
    queries,
    key_vectors,
    value_vectors,
    frozen_grad,
    output_grad,
    document_ids,
    document_tenant,
    tenant_owner,
    phm_rule,
    phm_left,
    phm_right,
):
    rows = queries.shape[0]
    reach = (WINDOW + rows - 2) // rows
    seq_count = lax.axis_size("seq")
    head_count = lax.axis_size("head")
    seq_index = lax.axis_index("seq")
    head_index = lax.axis_index("head")
    tenants = tenant_owner.shape[0]
    block_count = PHM_N // head_count
    block_start = head_index * block_count
    factor_columns = tenants * PHM_N
    sub_left, sub_right = phm_left.shape[2], phm_right.shape[2]

    distances = list(range(reach, 0, -1))
    keys = [passed_along(key_vectors, "seq", d) for d in distances] + [key_vectors]
    values = [passed_along(value_vectors, "seq", d) for d in distances] + [value_vectors]

    slots = jnp.arange(tenants, dtype=jnp.int32)
    owner_hot = tenant_owner[None, :] == slots[:, None]

    def by_owner(array):
        hot = owner_hot.reshape((tenants, tenants) + (1,) * (array.ndim - 1))
        return jnp.sum(jnp.where(hot, array[None], 0.0), axis=1)

    rule = by_owner(phm_rule).reshape(factor_columns, PHM_N, PHM_N)
    left = by_owner(phm_left).reshape(factor_columns, sub_left)
    right = by_owner(phm_right).reshape(factor_columns, sub_right)

    lead = jnp.full((reach * rows,), -1, jnp.int32)
    key_docs = lax.dynamic_slice_in_dim(
        jnp.concatenate([lead, document_ids]), seq_index * rows, (reach + 1) * rows
    )
    query_docs = key_docs[reach * rows :]
    document_owner = jnp.sum(
        jnp.where(document_tenant[:, None] == slots[None, :], tenant_owner[None, :], 0), axis=1
    )
    documents = jnp.arange(document_tenant.shape[0], dtype=jnp.int32)
    token_owner = jnp.sum(
        jnp.where(query_docs[:, None] == documents[None, :], document_owner[None, :], 0), axis=1
    )
    qinfo = jnp.stack([query_docs, token_owner], axis=1)
    column_owner = jnp.arange(factor_columns, dtype=jnp.int32) // PHM_N
    token_mask = token_owner[:, None] == column_owner[None, :]

    shifted = jnp.concatenate(
        [
            jnp.pad(right, ((0, 0), (b * sub_right, (block_count - 1 - b) * sub_right)))
            for b in range(block_count)
        ],
        axis=0,
    )
    shifted_hi, shifted_lo = split_two(shifted)
    gate_both = dot_nt(output_grad, jnp.concatenate([shifted_hi, shifted_lo], axis=0))
    wide = block_count * factor_columns
    gate_sum = gate_both[:, :wide] + gate_both[:, wide:]
    gate_here = jnp.stack(
        [
            jnp.where(token_mask, gate_sum[:, b * factor_columns : (b + 1) * factor_columns], 0.0)
            for b in range(block_count)
        ]
    )
    gate = lax.all_gather(gate_here, "head", axis=0, tiled=True)

    rule_abc = rule.transpose(1, 2, 0)
    rule_rows = lax.dynamic_slice_in_dim(rule_abc, block_start, block_count, 0)
    rule_cols = lax.dynamic_slice_in_dim(rule_abc, block_start, block_count, 1)
    left_hi, left_lo = split_two(left)
    results = attention(
        queries, frozen_grad, keys, values, gate, qinfo, key_docs[None, :], rule_rows,
        left_hi, left_lo, block_count,
    )
    query_grad, own_terms = results[0], results[1]
    back = results[2 : 2 + reach]
    proj_here, left_sum = results[2 + reach :]
    returned = [passed_along(back[j], "seq", -(reach - j)) for j in range(reach)]

    proj = lax.all_gather(proj_here, "head", axis=0, tiled=True)
    rule_proj = jnp.sum(proj[:, None] * rule_cols[:, :, None, :], axis=0)
    rule_proj = jnp.concatenate([rule_proj[b] for b in range(block_count)], axis=1)
    proj_hi, proj_lo = split_two(rule_proj)
    right_both = dot_tn(jnp.concatenate([proj_hi, proj_lo], axis=1), output_grad)
    right_wide = right_both[:wide] + right_both[wide:]
    right_sum = sum(
        right_wide[
            b * factor_columns : (b + 1) * factor_columns, b * sub_right : (b + 1) * sub_right
        ]
        for b in range(block_count)
    )
    rule_here = jnp.sum(proj_here[:, None] * gate[None], axis=2)
    rule_sum = lax.dynamic_update_slice_in_dim(
        jnp.zeros((PHM_N, PHM_N, factor_columns), f32), rule_here, block_start, 0
    ).transpose(2, 0, 1)

    count = seq_count * head_count
    grad_scale = rows ** (-0.5)
    flat = jnp.concatenate(
        [
            right_sum.reshape(count, -1),
            left_sum.reshape(count, -1),
            rule_sum.reshape(count, -1),
        ],
        axis=1,
    )
    size = flat.shape[1]
    padded = -(-size // 1024) * 1024
    pieces = jnp.pad(flat * grad_scale, ((0, 0), (0, padded - size)))
    summed = exchange_sum(pieces.reshape(count, padded // 128, 128), seq_count, head_count)
    summed = summed.reshape(-1)
    factors = PHM_N // head_count
    right_end = factors * sub_right
    left_end = right_end + factors * sub_left
    right_grad = summed[:right_end].reshape(1, factors, sub_right)
    left_grad = summed[right_end:left_end].reshape(1, factors, sub_left)
    rule_grad = summed[left_end:size].reshape(1, factors, PHM_N, PHM_N)

    terms = own_terms
    for received in returned:
        terms = terms + received.astype(f32)
    key_grad = terms[0].astype(bf16)
    value_grad = terms[1].astype(bf16)
    return (query_grad, key_grad, value_grad, rule_grad, left_grad, right_grad)


def solution(mesh):
    rows = P(("groups", "seq"), "head")
    in_specs = (
        rows, rows, rows, rows, rows,
        P("groups"),
        P("groups"),
        P(),
        P("groups", None, None, None),
        P("groups", None, None),
        P("groups", None, None),
    )
    out_specs = (
        rows, rows, rows,
        P(("groups", "seq"), "head", None, None),
        P(("groups", "seq"), "head", None),
        P(("groups", "seq"), "head", None),
    )
    return jax.shard_map(
        on_device, mesh=mesh, in_specs=in_specs, out_specs=out_specs, check_vma=False
    )
```

time: 316 us -> 146 us (0.46); the launches traced: 311 us -> 144 us
  blocking collectives: 114 us -> 4.13 us
  matrix products: 79.3 us -> 0.93 us
  Pallas kernels: 0 us -> 73.8 us
  other arithmetic: 28.6 us -> 10.7 us
  local copies, waits for them, and re-layouts: 52.3 us -> 35.8 us
  between operations: 15.2 us -> 0.9 us
  starting transfers between devices: 21.5 us -> 18.1 us
    unnamed x1 -> x0, blocking collectives: 110 us -> none
    dot_general x34 -> x2, matrix products: 79.1 us -> 0.93 us  [the longest x1 0.57 us: dot_nt(): lax.dot_general(a, b, (((1,), (1,)), ((), ())), preferred_element_type=f32)]
    pallas_call x0 -> x2, Pallas kernels: none -> 73.8 us  [the longest x1 59.8 us: exchange_sum(): pl.pallas_call(functools.partial(exchange_kernel, seq_count, head_count),...]
    gather x4 -> x0, local copies, waits for them, and re-layouts: 11.8 us -> none  [the longest x1 6.18 us: on_device(): right_tok = phm_right[tenant]]
    unnamed x89 -> x38, local copies, waits for them, and re-layouts: 24.4 us -> 16 us
    sub x4 -> x0, other arithmetic: 6.43 us -> none  [attend(): expo_terms = jnp.exp(scores - row_max)]
    convert_element_type x7 -> x3, other arithmetic: 7.3 us -> 1.15 us  [split_two(): return (high.astype(bf16), (value - high).astype(bf16))]
    dot_general x2 -> x0, other arithmetic: 5.69 us -> none  [the longest x1 4.07 us: on_device(): jnp.einsum('tia,tiab->tib', left_proj, rule_cols, precision=highest)]
  transfers between devices with their start and end apart: 9 -> 6, of which waited for: 0 -> 0; matrix products, arithmetic and copies ran while one was open for 38% -> 19% of each run, Pallas kernels for 0% -> 41%
where the time goes in v1:
time: 146 us; the launch traced here: 144 us
  Pallas kernels  73.8 us (51%)
  local copies, waits for them, and re-layouts  35.8 us (25%)
  starting transfers between devices  18.1 us (12%)
  other arithmetic  10.7 us (7%)
  blocking collectives  4.13 us (3%)
    pallas_call x1, Pallas kernels, exchange_sum(): pl.pallas_call(functools.partial(exchange_kernel, seq_count, head_count),...  59.8 us
    ppermute x6, starting transfers between devices, passed_along(): lax.ppermute(value, axis, [(source, source + steps) for source in range(f...  18.1 us
    unnamed x38, local copies, waits for them, and re-layouts  16 us
    pallas_call x1, Pallas kernels, attention(): pl.pallas_call(functools.partial(attention_kernel, reach, heads_per_block...  14 us
  transfers between devices with their start and end apart: 6, of which 0 were waited for; matrix products, arithmetic and copies ran while one was open for 19% of the time, Pallas kernels for 41%

profile of v1, /device:TPU:0, one launch (start us, length us, event | category | flops | bytes accessed | tf_op | source)
XLA Modules:
  0.0 144.3 jit_solution(7510137334698276295)
XLA Ops:
  0.6 0.0 copy-start
  0.6 5.1 %collective-permute-start = (bf16[256,1024]{1,0:T(8,128)(2,1)}, bf16[256,1024]{1,0:T(8,128)(2,1)S(1)}, u32[]{:S(2)}, u32[]{:S(2)}) collective-permute-start(bf16[256,1024]{1,0:T(8,128)(2,1)} %refs_4_.1), channel_id=1, source_target_pairs={{0,4},{2,6},{4,8},{6,10},{8,12},{10,14},{1,5},{3,7},{5,9},{7,11},{... | collective-permute-start | bytes 1572872 | tf_op jit(solution)/shard_map/ppermute | solution.py:24
  5.7 3.5 %collective-permute-start.1 = (bf16[256,1024]{1,0:T(8,128)(2,1)}, bf16[256,1024]{1,0:T(8,128)(2,1)S(1)}, u32[]{:S(2)}, u32[]{:S(2)}) collective-permute-start(bf16[256,1024]{1,0:T(8,128)(2,1)} %refs_4_.1), channel_id=1, source_target_pairs={{0,2},{2,4},{4,6},{6,8},{8,10},{10,12},{12,14},{1,3},{3,5},{5,7},{... | collective-permute-start | bytes 1572872 | tf_op jit(solution)/shard_map/ppermute | solution.py:24
  9.2 3.5 %collective-permute-start.2 = (bf16[256,1024]{1,0:T(8,128)(2,1)}, bf16[256,1024]{1,0:T(8,128)(2,1)S(1)}, u32[]{:S(2)}, u32[]{:S(2)}) collective-permute-start(bf16[256,1024]{1,0:T(8,128)(2,1)} %refs_7_.1), channel_id=1, source_target_pairs={{0,4},{2,6},{4,8},{6,10},{8,12},{10,14},{1,5},{3,7},{5,9},{7,11},{... | collective-permute-start | bytes 1572872 | tf_op jit(solution)/shard_map/ppermute | solution.py:24
  12.7 3.5 %collective-permute-start.3 = (bf16[256,1024]{1,0:T(8,128)(2,1)}, bf16[256,1024]{1,0:T(8,128)(2,1)S(1)}, u32[]{:S(2)}, u32[]{:S(2)}) collective-permute-start(bf16[256,1024]{1,0:T(8,128)(2,1)} %refs_7_.1), channel_id=1, source_target_pairs={{0,2},{2,4},{4,6},{6,8},{8,10},{10,12},{12,14},{1,3},{3,5},{5,7},{... | collective-permute-start | bytes 1572872 | tf_op jit(solution)/shard_map/ppermute | solution.py:24
  16.2 0.8 pad_dynamic-slice_fusion
  17.0 0.7 iota_compare_fusion.3
  17.6 0.9 select_reduce_fusion.4
  18.5 0.9 copy.29
  19.4 1.2 select_reduce_fusion
  20.6 1.7 %reshape.109 = f32[32,1344]{1,0:T(8,128)} reshape(f32[8,4,1344]{2,1,0:T(4,128)} %select_reduce_fusion) | data formatting | bytes 344064 | tf_op jit(solution)/shard_map/reshape | solution.py:265
  22.2 1.1 reduce-precision_convert_fusion
  23.4 0.6 convolution_bitcast_fusion
  24.0 0.1 select_reduce_fusion.3
  24.1 0.1 fusion.10
  24.2 2.0 %all_gather.6 = f32[4,256,32]{1,2,0:T(8,128)} all-gather(f32[2,256,32]{1,2,0:T(8,128)S(1)} %pad_maximum_fusion), channel_id=1, replica_groups=mesh['groups'=2,'seq'=8,'head'=2] {'head'}, dimensions={0}, use_global_device_ids=true | all-gather | bytes 196608 | tf_op jit(solution)/shard_map/all_gather | solution.py:300
  26.2 1.9 %copy.32.refs_8_ = f32[4,256,32]{2,1,0:T(8,128)} copy(f32[4,256,32]{1,2,0:T(8,128)} %all_gather.6) | data formatting | bytes 262144 | tf_op jit(solution)/shard_map/all_gather | solution.py:300
  28.1 0.8 copy.33.refs_9_
  28.9 0.8 select_reduce_fusion.2
  29.7 0.9 copy.30
  30.6 0.1 reshape.110
  30.7 0.9 copy.31
  31.6 0.9 select_reduce_fusion.1
  32.4 0.9 reshape.111
  33.4 0.8 copy-done.8
  34.2 0.8 copy-done.10
  35.0 0.8 copy-done.12
  35.8 0.8 copy-done.14
  36.5 1.0 copy-done.1
  37.6 0.9 copy-done.3
  38.5 1.0 copy-done.4
  39.5 1.0 copy-done.5
  40.6 1.0 copy-done.6
  41.6 1.0 copy-done.7
  42.7 1.0 copy-done.9
  43.7 1.0 copy-done.11
  44.7 1.0 copy-done.13
  45.8 1.0 copy-done.15
  46.8 14.0 %shard_map.154 = (bf16[256,1024]{1,0:T(8,128)(2,1)}, f32[2,256,1024]{2,1,0:T(8,128)S(1)}, bf16[2,256,1024]{2,1,0:T(8,128)(2,1)}, bf16[2,256,1024]{2,1,0:T(8,128)...) custom-call(bf16[256,1024]{1,0:T(8,128)(2,1)S(1)} %copy-done.4, bf16[256,1024]{1,0:T(8,128)(2,1)S(1)} %copy-done.5, ...), custom_call_target="tpu_custom_call" | custom-call | flops 2415919104 | bytes 10485760 | tf_op jit(solution)/shard_map/pallas_call | solution.py:145
  60.8 0.7 copy-done.2
  61.5 1.7 %copy.34 = f32[2,256,32]{1,2,0:T(8,128)} copy(f32[2,256,32]{2,1,0:T(8,128)} %copy-done.2) | data formatting | bytes 131072 | tf_op jit(solution)/shard_map/pallas_call | solution.py:145
  63.2 2.1 %all_gather.7 = f32[4,256,32]{1,2,0:T(8,128)S(1)} all-gather(f32[2,256,32]{1,2,0:T(8,128)} %copy.34), channel_id=1, replica_groups=mesh['groups'=2,'seq'=8,'head'=2] {'head'}, dimensions={0}, use_global_device_ids=true | all-gather | bytes 196608 | tf_op jit(solution)/shard_map/all_gather | solution.py:315
  65.3 0.1 multiply_reduce_fusion.1
  65.4 0.4 fusion.6
  65.8 0.1 slice_add_fusion
  65.9 1.3 collective-permute-start.4
  67.2 1.3 collective-permute-start.5
  68.5 0.8 slice_add_fusion.1
  69.3 1.7 %reshape.112 = f32[16,2688]{1,0:T(8,128)} reshape(f32[32,1344]{1,0:T(8,128)} %slice_add_fusion.1) | data formatting | bytes 344064 | tf_op jit(solution)/shard_map/reshape | solution.py:336
  71.0 1.0 multiply_reduce_fusion
  72.0 0.7 copy.36
  72.7 0.6 broadcast_in_dim.134
  73.3 1.4 constant_dynamic-update-slice_fusion
  74.7 0.9 reshape.114
  75.6 0.7 reshape.113
  76.3 1.0 maximum_multiply_fusion
  77.3 0.1 copy.37
  77.4 59.8 %shard_map.155 = f32[32,128]{1,0:T(8,128)S(1)} custom-call(f32[16,32,128]{2,1,0:T(8,128)S(1)} %bitcast.30), custom_call_target="tpu_custom_call" | custom-call | flops 65536 | bytes 524288 | tf_op jit(solution)/shard_map/pallas_call | solution.py:208
  137.2 1.5 %slice.68 = f32[128,2,4,4]{3,2,1,0:T(4,128)} reshape(f32[32,128]{1,0:T(8,128)S(1)} %shard_map.155) | data formatting | bytes 32768 | tf_op jit(solution)/shard_map/slice | solution.py:352
  138.7 1.3 slice.84
  139.9 0.7 reshape.117
  140.6 0.6 reshape.116
  141.2 2.0 %add_convert_fusion = bf16[2,256,1024]{2,1,0:T(8,128)(2,1)S(1)} fusion(bf16[2,256,1024]{2,1,0:T(8,128)(2,1)} %collective-permute-done.5, f32[2,256,1024]{2,1,0:T(8,128)S(1)} %get-tuple-element.13, bf16[2,256,1024]{2,1,0:T(8,128)(2,1)} %collective-permute-done.4), kind=kLoop, calls=%fused_computation | loop fusion | flops 2621440 | bytes 5242880 | tf_op jit(solution)/shard_map/convert.1
  143.3 1.0 slice_bitcast_fusion
  (38 shorter events, 0.2 us)
Async XLA Ops:
  0.6 22.7 %copy-start = (bf16[256,2688]{1,0:T(8,128)(2,1)S(1)}, bf16[256,2688]{1,0:T(8,128)(2,1)}, u32[]{:S(2)}) copy-start(bf16[256,2688]{1,0:T(8,128)(2,1)} %param.15) | copy-start | bytes 4128772
  0.6 32.7 %collective-permute-start = (bf16[256,1024]{1,0:T(8,128)(2,1)}, bf16[256,1024]{1,0:T(8,128)(2,1)S(1)}, u32[]{:S(2)}, u32[]{:S(2)}) collective-permute-start(bf16[256,1024]{1,0:T(8,128)(2,1)} %refs_4_.1), channel_id=1, source_target_pairs={{0,4},{2,6},{4,8},{6,10},{8,12},{10,14},{1,5},{3,7},{5,9},{7,11},{... | collective-permute-start | bytes 1572872 | tf_op jit(solution)/shard_map/ppermute | solution.py:24
  5.7 28.4 %collective-permute-start.1 = (bf16[256,1024]{1,0:T(8,128)(2,1)}, bf16[256,1024]{1,0:T(8,128)(2,1)S(1)}, u32[]{:S(2)}, u32[]{:S(2)}) collective-permute-start(bf16[256,1024]{1,0:T(8,128)(2,1)} %refs_4_.1), channel_id=1, source_target_pairs={{0,2},{2,4},{4,6},{6,8},{8,10},{10,12},{12,14},{1,3},{3,5},{5,7},{... | collective-permute-start | bytes 1572872 | tf_op jit(solution)/shard_map/ppermute | solution.py:24
  9.2 25.7 %collective-permute-start.2 = (bf16[256,1024]{1,0:T(8,128)(2,1)}, bf16[256,1024]{1,0:T(8,128)(2,1)S(1)}, u32[]{:S(2)}, u32[]{:S(2)}) collective-permute-start(bf16[256,1024]{1,0:T(8,128)(2,1)} %refs_7_.1), channel_id=1, source_target_pairs={{0,4},{2,6},{4,8},{6,10},{8,12},{10,14},{1,5},{3,7},{5,9},{7,11},{... | collective-permute-start | bytes 1572872 | tf_op jit(solution)/shard_map/ppermute | solution.py:24
  12.7 23.1 %collective-permute-start.3 = (bf16[256,1024]{1,0:T(8,128)(2,1)}, bf16[256,1024]{1,0:T(8,128)(2,1)S(1)}, u32[]{:S(2)}, u32[]{:S(2)}) collective-permute-start(bf16[256,1024]{1,0:T(8,128)(2,1)} %refs_7_.1), channel_id=1, source_target_pairs={{0,2},{2,4},{4,6},{6,8},{8,10},{10,12},{12,14},{1,3},{3,5},{5,7},{... | collective-permute-start | bytes 1572872 | tf_op jit(solution)/shard_map/ppermute | solution.py:24
  23.4 5.5 %copy-start.16 = (f32[8,4,4,4]{0,3,2,1:T(4,128)S(1)}, f32[8,4,4,4]{0,3,2,1:T(4,128)}, u32[]{:S(2)}) copy-start(f32[8,4,4,4]{0,3,2,1:T(4,128)} %param.19) | copy-start | bytes 6148
  33.4 0.8 copy-start.8
  34.2 0.8 copy-start.10
  35.0 0.8 copy-start.12
  35.7 0.8 copy-start.14
  36.5 1.0 copy-start.1
  37.6 0.9 copy-start.3
  38.5 1.0 copy-start.4
  39.5 1.0 copy-start.5
  40.6 1.0 copy-start.6
  41.6 1.0 copy-start.7
  42.7 1.0 copy-start.9
  43.7 1.0 copy-start.11
  44.7 1.0 copy-start.13
  45.8 1.0 copy-start.15
  60.8 0.7 copy-start.2
  65.9 75.3 %collective-permute-start.4 = (bf16[2,256,1024]{2,1,0:T(8,128)(2,1)}, bf16[2,256,1024]{2,1,0:T(8,128)(2,1)}, u32[]{:S(2)}, u32[]{:S(2)}) collective-permute-start(bf16[2,256,1024]{2,1,0:T(8,128)(2,1)} %get-tuple-element.14), channel_id=1, source_target_pairs={{4,0},{6,2},{8,4},{10,6},{12,8},{14,10},{5,1},{7,3},{9,5},{11,7},{... | collective-permute-start | bytes 3145736 | tf_op jit(solution)/shard_map/ppermute | solution.py:24
  67.2 74.0 %collective-permute-start.5 = (bf16[2,256,1024]{2,1,0:T(8,128)(2,1)}, bf16[2,256,1024]{2,1,0:T(8,128)(2,1)}, u32[]{:S(2)}, u32[]{:S(2)}) collective-permute-start(bf16[2,256,1024]{2,1,0:T(8,128)(2,1)} %get-tuple-element.15), channel_id=1, source_target_pairs={{2,0},{4,2},{6,4},{8,6},{10,8},{12,10},{14,12},{3,1},{5,3},{7,5},{... | collective-permute-start | bytes 3145736 | tf_op jit(solution)/shard_map/ppermute | solution.py:24

commit v2 on v1

v2 whole, which is shorter than its diff:
```python
import functools

import jax
import jax.numpy as jnp
from jax import lax
from jax.experimental import pallas as pl
from jax.experimental.pallas import tpu as pltpu
from jax.sharding import PartitionSpec as P

HEAD_DIM = 128
WINDOW = 512
PHM_N = 4
MESH = pl.DeviceIdType.MESH

score_scale = 168.0 ** (-0.5)
neg_big = -1e30
f32 = jnp.float32
bf16 = jnp.bfloat16


def split_two(value):
    high = lax.reduce_precision(value, 8, 7)
    return high.astype(bf16), (value - high).astype(bf16)


def kernel_split(value):
    high = value.astype(bf16)
    return high, (value - high.astype(f32)).astype(bf16)


def dot_nt(a, b):
    return lax.dot_general(a, b, (((1,), (1,)), ((), ())), preferred_element_type=f32)


def dot_nn(a, b):
    return lax.dot_general(a, b, (((1,), (0,)), ((), ())), preferred_element_type=f32)


def dot_tn(a, b):
    return lax.dot_general(a, b, (((0,), (0,)), ((), ())), preferred_element_type=f32)


def main_kernel(reach, seq_count, head_count, *refs):
    (q_ref, k_ref, v_ref, frozen_ref, og_ref, gate_par_ref, qinfo_ref, kdoc_ref, rule_ref, lhi_ref, llo_ref,
     dq_ref, dk_ref, dv_ref, left_ref, right_ref, rule_out_ref,
     kv_land, back_out, back_land, own_ref, bias_ref, gate_ref, proj_ref,
     kv_send, kv_recv, back_send, back_recv, pair_send, pair_recv) = refs
    rows, width = q_ref.shape
    heads = width // HEAD_DIM
    blocks = reach + 1
    block_count = PHM_N // head_count
    heads_per_block = heads // block_count
    columns = gate_ref.shape[2]
    s = lax.axis_index("seq")
    me = lax.axis_index("head")
    mine = me * block_count
    distances = range(1, reach + 1)

    def span(h):
        return pl.ds(pl.multiple_of(h * HEAD_DIM, HEAD_DIM), HEAD_DIM)

    barrier = pltpu.get_barrier_semaphore()
    for d in distances:
        @pl.when(s + d < seq_count)
        def _():
            pl.semaphore_signal(barrier, inc=1, device_id={"seq": s + d}, device_id_type=MESH)

        @pl.when(s >= d)
        def _():
            pl.semaphore_signal(barrier, inc=1, device_id={"seq": s - d}, device_id_type=MESH)

    for step in range(1, head_count):
        pl.semaphore_signal(
            barrier, inc=1, device_id={"head": lax.rem(me + step, head_count)}, device_id_type=MESH
        )
    pl.semaphore_wait(
        barrier,
        jnp.minimum(s, reach) + jnp.minimum(seq_count - 1 - s, reach) + (head_count - 1),
    )

    def kv_copy(h, d, which):
        source = (k_ref, v_ref)[which]
        return pltpu.make_async_remote_copy(
            src_ref=source.at[:, span(h)],
            dst_ref=kv_land.at[d - 1, which, h],
            send_sem=kv_send.at[d - 1, which, h],
            recv_sem=kv_recv.at[d - 1, which, h],
            device_id={"seq": lax.rem(s + d, seq_count)},
            device_id_type=MESH,
        )

    def back_copy(h, d, which):
        return pltpu.make_async_remote_copy(
            src_ref=back_out.at[d - 1, which, h],
            dst_ref=back_land.at[d - 1, which, h],
            send_sem=back_send.at[d - 1, which, h],
            recv_sem=back_recv.at[d - 1, which, h],
            device_id={"seq": lax.rem(s - d + seq_count, seq_count)},
            device_id_type=MESH,
        )

    def pair_copy(buffer, index, step):
        return pltpu.make_async_remote_copy(
            src_ref=buffer.at[pl.ds(mine, block_count)],
            dst_ref=buffer.at[pl.ds(mine, block_count)],
            send_sem=pair_send.at[index, step],
            recv_sem=pair_recv.at[index, step],
            device_id={"head": lax.rem(me + step, head_count)},
            device_id_type=MESH,
        )

    def each(body):
        def step(h, carry):
            body(h)
            return carry

        lax.fori_loop(0, heads, step, 0)

    def for_pairs(condition, act):
        def body(h):
            for d in distances:
                @pl.when(condition(d))
                def _():
                    for which in range(2):
                        act(h, d, which)

        each(body)

    sends = lambda d: s + d < seq_count
    takes = lambda d: s >= d
    for_pairs(sends, lambda h, d, w: kv_copy(h, d, w).start())
    for d in distances:
        @pl.when(s < d)
        def _():
            kv_land[d - 1] = jnp.zeros(kv_land.shape[1:], bf16)

    slot = lax.broadcasted_iota(jnp.int32, (rows, columns), 1) // PHM_N
    mask = slot == qinfo_ref[:, 1:2]
    gate_both = dot_nt(og_ref[...], gate_par_ref[...])
    wide = block_count * columns
    for b in range(block_count):
        total = (
            gate_both[:, b * columns : (b + 1) * columns]
            + gate_both[:, wide + b * columns : wide + (b + 1) * columns]
        )
        gate_ref[mine + b] = jnp.where(mask, total, 0.0)
        proj_ref[mine + b] = jnp.zeros((rows, columns), f32)
    for step in range(1, head_count):
        pair_copy(gate_ref, 0, step).start()
    left_ref[...] = jnp.zeros_like(left_ref)
    query_pos = lax.broadcasted_iota(jnp.int32, (rows, rows), 0)
    key_pos = lax.broadcasted_iota(jnp.int32, (rows, rows), 1)
    for j in range(blocks):
        later = query_pos - key_pos + j * rows
        start = (reach - j) * rows
        same = qinfo_ref[:, 0:1] == kdoc_ref[:, start : start + rows]
        allowed = same & (later >= 0) & (later < WINDOW)
        bias_ref[j] = jnp.where(allowed, 0.0, neg_big)
    for step in range(1, head_count):
        pair_copy(gate_ref, 0, step).wait()

    def one_head(h):
        block = h // heads_per_block
        part_span = span(lax.rem(h, heads_per_block))
        mix = jnp.zeros((rows, columns), f32)
        for b in range(PHM_N):
            mix = mix + gate_ref[b] * rule_ref[mine + block, pl.ds(b, 1), :]
        mix_hi, mix_lo = kernel_split(mix)
        lhi = lhi_ref[:, part_span]
        llo = llo_ref[:, part_span]
        adapter = dot_nn(mix_hi, lhi) + dot_nn(mix_lo, lhi) + dot_nn(mix_hi, llo)
        cot = (frozen_ref[:, span(h)].astype(f32) + adapter).astype(bf16)
        q = q_ref[:, span(h)]
        for d in distances:
            @pl.when(takes(d))
            def _():
                for which in range(2):
                    kv_copy(h, d, which).wait_recv()

        keys = [k_ref[:, span(h)]] + [kv_land[d - 1, 0, h] for d in distances]
        values = [v_ref[:, span(h)]] + [kv_land[d - 1, 1, h] for d in distances]
        scores = [dot_nt(q, keys[j]) * score_scale + bias_ref[j] for j in range(blocks)]
        row_max = functools.reduce(jnp.maximum, [jnp.max(x, axis=1, keepdims=True) for x in scores])
        expo = [jnp.exp(x - row_max) for x in scores]
        total = functools.reduce(jnp.add, [jnp.sum(e, axis=1, keepdims=True) for e in expo])
        inverse = 1.0 / total
        prob = [e * inverse for e in expo]
        low = [p.astype(bf16) for p in prob]
        out = functools.reduce(jnp.add, [dot_nn(low[j], values[j]) for j in range(blocks)]).astype(bf16)
        grad = [dot_nt(cot, values[j]) for j in range(blocks)]
        row_dot = functools.reduce(
            jnp.add, [jnp.sum(prob[j] * grad[j], axis=1, keepdims=True) for j in range(blocks)]
        )
        dscore = [(prob[j] * (grad[j] - row_dot)).astype(bf16) for j in range(blocks)]
        for d in reversed(distances):
            back_out[d - 1, 0, h] = (dot_tn(dscore[d], q) * score_scale).astype(bf16)
            back_out[d - 1, 1, h] = dot_tn(low[d], cot).astype(bf16)

            @pl.when(takes(d))
            def _():
                for which in range(2):
                    back_copy(h, d, which).start()

        own_ref[0, h] = dot_tn(dscore[0], q) * score_scale
        own_ref[1, h] = dot_tn(low[0], cot)
        dq = functools.reduce(jnp.add, [dot_nn(dscore[j], keys[j]) for j in range(blocks)])
        dq_ref[:, span(h)] = (dq * score_scale).astype(bf16)
        proj = jnp.where(mask, dot_nt(out, lhi) + dot_nt(out, llo), 0.0)
        proj_ref[mine + block] += proj
        left_ref[:, part_span] += dot_tn(mix_hi, out) + dot_tn(mix_lo, out)

    each(one_head)

    for step in range(1, head_count):
        pair_copy(proj_ref, 1, step).start()
    for a in range(block_count):
        for b in range(PHM_N):
            rule_out_ref[a, b : b + 1, :] = jnp.sum(
                proj_ref[mine + a] * gate_ref[b], axis=0, keepdims=True
            )
    for step in range(1, head_count):
        pair_copy(proj_ref, 1, step).wait()
    for b in range(block_count):
        mixed = jnp.zeros((rows, columns), f32)
        for a in range(PHM_N):
            mixed = mixed + proj_ref[a] * rule_ref[a, pl.ds(mine + b, 1), :]
        high, low = kernel_split(mixed)
        og = og_ref[...]
        right_ref[b] = dot_tn(high, og) + dot_tn(low, og)

    def finish(h):
        for d in distances:
            @pl.when(sends(d))
            def _():
                for which in range(2):
                    back_copy(h, d, which).wait_recv()
                    own_ref[which, h] += back_land[d - 1, which, h].astype(f32)

        dk_ref[:, span(h)] = own_ref[0, h].astype(bf16)
        dv_ref[:, span(h)] = own_ref[1, h].astype(bf16)

    each(finish)
    for_pairs(sends, lambda h, d, w: kv_copy(h, d, w).wait_send())
    for_pairs(takes, lambda h, d, w: back_copy(h, d, w).wait_send())


def main_call(seq_count, head_count, reach, operands):
    queries, output_grad, lhi = operands[0], operands[4], operands[9]
    rows, width = queries.shape
    heads = width // HEAD_DIM
    columns = lhi.shape[0]
    block_count = PHM_N // head_count
    vmem = pl.BlockSpec(memory_space=pltpu.VMEM)
    wide = jax.ShapeDtypeStruct((rows, width), bf16)
    moved = (reach, 2, heads, rows, HEAD_DIM)
    dma = pltpu.SemaphoreType.DMA
    return pl.pallas_call(
        functools.partial(main_kernel, reach, seq_count, head_count),
        in_specs=[vmem] * len(operands),
        out_specs=[vmem] * 6,
        out_shape=[
            wide, wide, wide,
            jax.ShapeDtypeStruct(lhi.shape, f32),
            jax.ShapeDtypeStruct((block_count, columns, output_grad.shape[1]), f32),
            jax.ShapeDtypeStruct((block_count, PHM_N, columns), f32),
        ],
        scratch_shapes=[
            pltpu.VMEM(moved, bf16),
            pltpu.VMEM(moved, bf16),
            pltpu.VMEM(moved, bf16),
            pltpu.VMEM((2, heads, rows, HEAD_DIM), f32),
            pltpu.VMEM((reach + 1, rows, rows), f32),
            pltpu.VMEM((PHM_N, rows, columns), f32),
            pltpu.VMEM((PHM_N, rows, columns), f32),
            dma((reach, 2, heads)),
            dma((reach, 2, heads)),
            dma((reach, 2, heads)),
            dma((reach, 2, heads)),
            dma((2, head_count)),
            dma((2, head_count)),
        ],
        compiler_params=pltpu.CompilerParams(
            collective_id=1, has_side_effects=True, vmem_limit_bytes=48 * 2**20
        ),
    )(*operands)


def exchange_kernel(seq_count, head_count, x_ref, o_ref, landed, send_sem, recv_sem):
    count = seq_count * head_count
    me = lax.axis_index("seq") * head_count + lax.axis_index("head")

    def device(step):
        peer = lax.rem(me + step, count)
        return peer, {"seq": peer // head_count, "head": lax.rem(peer, head_count)}

    barrier = pltpu.get_barrier_semaphore()
    for step in range(1, count):
        pl.semaphore_signal(barrier, inc=1, device_id=device(step)[1], device_id_type=MESH)
    pl.semaphore_wait(barrier, count - 1)
    copies = []
    for step in range(1, count):
        peer, where = device(step)
        copy = pltpu.make_async_remote_copy(
            src_ref=x_ref.at[peer],
            dst_ref=landed.at[step],
            send_sem=send_sem.at[step],
            recv_sem=recv_sem.at[step],
            device_id=where,
            device_id_type=MESH,
        )
        copy.start()
        copies.append(copy)
    total = x_ref[me]
    for step in range(1, count):
        copies[step - 1].wait_recv()
        total = total + landed[step]
    o_ref[...] = total
    for copy in copies:
        copy.wait_send()


def exchange_sum(pieces, seq_count, head_count):
    count = seq_count * head_count
    return pl.pallas_call(
        functools.partial(exchange_kernel, seq_count, head_count),
        out_shape=jax.ShapeDtypeStruct(pieces.shape[1:], f32),
        in_specs=[pl.BlockSpec(memory_space=pltpu.VMEM)],
        out_specs=pl.BlockSpec(memory_space=pltpu.VMEM),
        scratch_shapes=[
            pltpu.VMEM(pieces.shape, f32),
            pltpu.SemaphoreType.DMA((count,)),
            pltpu.SemaphoreType.DMA((count,)),
        ],
        compiler_params=pltpu.CompilerParams(
            collective_id=0, has_side_effects=True, vmem_limit_bytes=32 * 2**20
        ),
        cost_estimate=pl.CostEstimate(
            flops=pieces.size, bytes_accessed=8 * pieces.size, transcendentals=0
        ),
    )(pieces)


def on_device(
    queries,
    key_vectors,
    value_vectors,
    frozen_grad,
    output_grad,
    document_ids,
    document_tenant,
    tenant_owner,
    phm_rule,
    phm_left,
    phm_right,
):
    rows = queries.shape[0]
    reach = (WINDOW + rows - 2) // rows
    seq_count = lax.axis_size("seq")
    head_count = lax.axis_size("head")
    seq_index = lax.axis_index("seq")
    head_index = lax.axis_index("head")
    tenants = tenant_owner.shape[0]
    block_count = PHM_N // head_count
    block_start = head_index * block_count
    factor_columns = tenants * PHM_N
    sub_left, sub_right = phm_left.shape[2], phm_right.shape[2]

    rule = phm_rule.transpose(2, 3, 0, 1).reshape(PHM_N, PHM_N, factor_columns)
    left = phm_left.reshape(factor_columns, sub_left)
    right = phm_right.reshape(factor_columns, sub_right)

    lead = jnp.full((reach * rows,), -1, jnp.int32)
    key_docs = lax.dynamic_slice_in_dim(
        jnp.concatenate([lead, document_ids]), seq_index * rows, (reach + 1) * rows
    )
    query_docs = key_docs[reach * rows :]
    documents = jnp.arange(document_tenant.shape[0], dtype=jnp.int32)
    token_tenant = jnp.sum(
        jnp.where(query_docs[:, None] == documents[None, :], document_tenant[None, :], 0), axis=1
    )
    qinfo = jnp.stack([query_docs, token_tenant], axis=1)

    shifted = jnp.concatenate(
        [
            jnp.pad(right, ((0, 0), (b * sub_right, (block_count - 1 - b) * sub_right)))
            for b in range(block_count)
        ],
        axis=0,
    )
    shifted_hi, shifted_lo = split_two(shifted)
    gate_params = jnp.concatenate([shifted_hi, shifted_lo], axis=0)
    left_hi, left_lo = split_two(left)
    query_grad, key_grad, value_grad, left_sum, right_both, rule_here = main_call(
        seq_count, head_count, reach,
        (queries, key_vectors, value_vectors, frozen_grad, output_grad, gate_params, qinfo,
         key_docs[None, :], rule, left_hi, left_lo),
    )
    right_sum = sum(
        right_both[b, :, b * sub_right : (b + 1) * sub_right] for b in range(block_count)
    )
    rule_sum = lax.dynamic_update_slice_in_dim(
        jnp.zeros((PHM_N, PHM_N, factor_columns), f32), rule_here, block_start, 0
    ).transpose(2, 0, 1)

    count = seq_count * head_count
    grad_scale = rows ** (-0.5)
    flat = jnp.concatenate(
        [
            right_sum.reshape(count, -1),
            left_sum.reshape(count, -1),
            rule_sum.reshape(count, -1),
        ],
        axis=1,
    )
    size = flat.shape[1]
    padded = -(-size // 1024) * 1024
    flat = jnp.pad(flat * grad_scale, ((0, 0), (0, padded - size)))
    slots = jnp.arange(tenants, dtype=jnp.int32)
    owner_hot = (tenant_owner[None, :] == slots[:, None])[:, :, None, None, None]
    rows_by_tenant = flat.reshape(1, tenants, head_count, padded // 128, 128)
    pieces = jnp.sum(jnp.where(owner_hot, rows_by_tenant, 0.0), axis=1)
    summed = exchange_sum(pieces.reshape(count, padded // 128, 128), seq_count, head_count)
    summed = summed.reshape(-1)
    factors = PHM_N // head_count
    right_end = factors * sub_right
    left_end = right_end + factors * sub_left
    right_grad = summed[:right_end].reshape(1, factors, sub_right)
    left_grad = summed[right_end:left_end].reshape(1, factors, sub_left)
    rule_grad = summed[left_end:size].reshape(1, factors, PHM_N, PHM_N)

    return (query_grad, key_grad, value_grad, rule_grad, left_grad, right_grad)


def solution(mesh):
    rows = P(("groups", "seq"), "head")
    in_specs = (
        rows, rows, rows, rows, rows,
        P("groups"),
        P("groups"),
        P(),
        P("groups", None, None, None),
        P("groups", None, None),
        P("groups", None, None),
    )
    out_specs = (
        rows, rows, rows,
        P(("groups", "seq"), "head", None, None),
        P(("groups", "seq"), "head", None),
        P(("groups", "seq"), "head", None),
    )
    return jax.shard_map(
        on_device, mesh=mesh, in_specs=in_specs, out_specs=out_specs, check_vma=False
    )
```

time: 146 us -> 83.4 us (0.57)
  local copies, waits for them, and re-layouts: 35.8 us -> 12.5 us
  starting transfers between devices: 18.1 us -> 0 us
  other arithmetic: 10.7 us -> 2.32 us
  Pallas kernels: 73.8 us -> 67.3 us
  blocking collectives: 4.13 us -> 0 us
    pallas_call x1, Pallas kernels: 59.8 us -> 10.4 us  [exchange_sum(): pl.pallas_call(functools.partial(exchange_kernel, seq_count, head_count),...]
    pallas_call x1, Pallas kernels: 14 us -> 57 us  [main_call(): pl.pallas_call(functools.partial(main_kernel, reach, seq_count, head_coun...]
    ppermute x6 -> x0, starting transfers between devices: 18.1 us -> none  [passed_along(): lax.ppermute(value, axis, [(source, source + steps) for source in range(f...]
    unnamed x38 -> x31, local copies, waits for them, and re-layouts: 16 us -> 6.51 us
    all_gather x2 -> x0, blocking collectives: 4.13 us -> none  [the longest x1 2.1 us: on_device(): proj = lax.all_gather(proj_here, 'head', axis=0, tiled=True)]
    reduce_sum x7 -> x2, other arithmetic: 4.87 us -> 0.98 us  [the longest x1 0.74 us: on_device(): jnp.sum(jnp.where(query_docs[:, None] == documents[None, :], document_ten...]
    reshape x4 -> x3, local copies, waits for them, and re-layouts: 4.29 us -> 1.1 us  [the longest x1 0.99 us: on_device(): right = phm_right.reshape(factor_columns, sub_right)]
    another operation x4 -> x1, other arithmetic: 2.14 us -> 0.01 us  [on_device(): qinfo = jnp.stack([query_docs, token_tenant], axis=1)]
  transfers between devices with their start and end apart: 6 -> 0, of which waited for: 0 -> 0; matrix products, arithmetic and copies ran while one was open for 19% -> 0% of each run, Pallas kernels for 41% -> 0%
where the time goes in v2:
time: 83.4 us; the launch traced here: 83 us
  Pallas kernels  67.3 us (81%)
  local copies, waits for them, and re-layouts  12.5 us (15%)
  other arithmetic  2.32 us (3%)
  between operations  0.89 us (1%)
    pallas_call x1, Pallas kernels, main_call(): pl.pallas_call(functools.partial(main_kernel, reach, seq_count, head_coun...  57 us
    pallas_call x1, Pallas kernels, exchange_sum(): pl.pallas_call(functools.partial(exchange_kernel, seq_count, head_count),...  10.4 us
    unnamed x31, local copies, waits for them, and re-layouts  6.51 us

profile of v2, /device:TPU:0, one launch (start us, length us, event | category | flops | bytes accessed | tf_op | source)
XLA Modules:
  0.0 83.0 jit_solution(1567891834837911860)
XLA Ops:
  0.6 0.8 pad_dynamic-slice_fusion
  1.4 0.7 select_reduce_fusion.1
  2.2 0.0 copy-start.10
  2.2 0.1 copy.26.refs_6_
  2.3 0.0 copy-start.11
  2.3 1.0 %reshape.70 = f32[32,1344]{1,0:T(8,128)S(1)} reshape(f32[8,4,1344]{2,1,0:T(4,128)} %param.21) | data formatting | bytes 344064 | tf_op jit(solution)/shard_map/reshape | solution.py:370
  3.3 0.0 copy-start
  3.3 0.0 copy-start.1
  3.4 0.0 copy-start.2
  3.4 0.0 copy-start.3
  3.4 0.1 reduce-precision_convert_fusion
  3.5 0.1 pad_maximum_fusion.refs_5_
  3.6 0.0 copy-done.10
  3.6 0.0 copy-done.11
  3.6 0.2 copy.25
  3.8 0.1 reshape.71.refs_8_
  3.9 0.5 copy-done
  4.4 0.2 copy-done.1
  4.5 0.2 copy-done.2
  4.7 0.2 copy-done.3
  4.9 57.0 %shard_map.154 = (bf16[256,1024]{1,0:T(8,128)(2,1)S(1)}, bf16[256,1024]{1,0:T(8,128)(2,1)S(1)}, bf16[256,1024]{1,0:T(8,128)(2,1)S(1)}, f32[32,512]{1,0:T(8,128)S...) custom-call(bf16[256,1024]{1,0:T(8,128)(2,1)S(1)} %copy-done, bf16[256,1024]{1,0:T(8,128)(2,1)S(1)} %copy-done.1, ...), custom_call_target="tpu_custom_call" | custom-call | tf_op jit(solution)/shard_map/pallas_call | solution.py:257
  61.8 0.0 copy-start.4
  61.8 0.8 copy-done.4
  62.6 0.0 copy-start.6
  62.6 0.8 copy-done.6
  63.4 0.0 copy-start.8
  63.4 0.8 %copy-done.8 = f32[2,32,2688]{2,1,0:T(8,128)} copy-done((f32[2,32,2688]{2,1,0:T(8,128)}, f32[2,32,2688]{2,1,0:T(8,128)S(1)}, u32[]{:S(2)}) %copy-start.8) | copy-done | bytes 688152
  64.3 0.0 copy-start.9
  64.3 0.6 copy-done.9
  64.9 0.1 copy.27
  65.0 0.0 copy-start.12
  65.1 0.1 reshape.74
  65.2 1.1 %slice_add_fusion = f32[1,32,1344]{2,1,0:T(8,128)S(1)} fusion(f32[2,32,2688]{2,1,0:T(8,128)} %copy-done.8), kind=kLoop, calls=%fused_computation.10 | loop fusion | flops 43008 | bytes 516096 | tf_op jit(solution)/shard_map/add | solution.py:398
  66.3 0.1 add.23
  66.4 0.9 %reshape.73 = f32[16,1024]{1,0:T(8,128)S(1)} reshape(f32[32,512]{1,0:T(8,128)} %copy-done.9) | data formatting | bytes 131072 | tf_op jit(solution)/shard_map/reshape | solution.py:410
  67.2 0.0 copy-start.7
  67.3 0.0 copy-start.5
  67.3 0.1 copy.28
  67.4 0.0 copy-done.12
  67.4 0.2 select_reduce_fusion
  67.7 10.4 %shard_map.155 = f32[32,128]{1,0:T(8,128)S(1)} custom-call(f32[16,32,128]{2,1,0:T(8,128)S(1)} %bitcast.11), custom_call_target="tpu_custom_call" | custom-call | flops 65536 | bytes 524288 | tf_op jit(solution)/shard_map/pallas_call | solution.py:324
  78.0 0.7 slice.26
  78.7 0.6 slice.30
  79.3 0.7 reshape.77
  80.0 0.6 reshape.76
  80.6 0.0 copy-done.7
  80.6 0.8 copy.33
  81.4 0.0 copy-done.5
  81.4 0.8 copy.34
  82.2 0.8 copy.35
  (12 shorter events, 0.1 us)
Async XLA Ops:
  2.2 1.4 %copy-start.10 = (f32[8,4,512]{2,1,0:T(4,128)S(1)}, f32[8,4,512]{2,1,0:T(4,128)}, u32[]{:S(2)}) copy-start(f32[8,4,512]{2,1,0:T(4,128)} %param.20) | copy-start | bytes 196612
  2.3 1.3 %copy-start.11 = (f32[8,4,4,4]{0,3,2,1:T(4,128)S(1)}, f32[8,4,4,4]{0,3,2,1:T(4,128)}, u32[]{:S(2)}) copy-start(f32[8,4,4,4]{0,3,2,1:T(4,128)} %param.19) | copy-start | bytes 6148
  3.3 1.0 %copy-start = (bf16[256,1024]{1,0:T(8,128)(2,1)S(1)}, bf16[256,1024]{1,0:T(8,128)(2,1)}, u32[]{:S(2)}) copy-start(bf16[256,1024]{1,0:T(8,128)(2,1)} %refs_0_.1) | copy-start | bytes 1572868
  3.3 1.2 %copy-start.1 = (bf16[256,1024]{1,0:T(8,128)(2,1)S(1)}, bf16[256,1024]{1,0:T(8,128)(2,1)}, u32[]{:S(2)}) copy-start(bf16[256,1024]{1,0:T(8,128)(2,1)} %refs_1_.1) | copy-start | bytes 1572868
  3.4 1.3 %copy-start.2 = (bf16[256,1024]{1,0:T(8,128)(2,1)S(1)}, bf16[256,1024]{1,0:T(8,128)(2,1)}, u32[]{:S(2)}) copy-start(bf16[256,1024]{1,0:T(8,128)(2,1)} %refs_2_.1) | copy-start | bytes 1572868
  3.4 1.5 %copy-start.3 = (bf16[256,1024]{1,0:T(8,128)(2,1)S(1)}, bf16[256,1024]{1,0:T(8,128)(2,1)}, u32[]{:S(2)}) copy-start(bf16[256,1024]{1,0:T(8,128)(2,1)} %refs_3_.1) | copy-start | bytes 1572868
  61.8 0.8 copy-start.4
  62.6 0.8 copy-start.6
  63.4 0.8 %copy-start.8 = (f32[2,32,2688]{2,1,0:T(8,128)}, f32[2,32,2688]{2,1,0:T(8,128)S(1)}, u32[]{:S(2)}) copy-start(f32[2,32,2688]{2,1,0:T(8,128)S(1)} %get-tuple-element.15) | copy-start | bytes 2064388
  64.3 0.6 copy-start.9
  65.0 2.4 %copy-start.12 = (s32[8]{0:T(128)S(1)}, s32[8]{0:T(128)}, u32[]{:S(2)}) copy-start(s32[8]{0:T(128)} %param.18) | copy-start | bytes 100
  67.2 13.4 %copy-start.7 = (bf16[256,1024]{1,0:T(8,128)(2,1)S(1)}, bf16[256,1024]{1,0:T(8,128)(2,1)}, u32[]{:S(2)}) copy-start(bf16[256,1024]{1,0:T(8,128)(2,1)} %copy-done.6) | copy-start | bytes 1572868
  67.3 14.1 %copy-start.5 = (bf16[256,1024]{1,0:T(8,128)(2,1)S(1)}, bf16[256,1024]{1,0:T(8,128)(2,1)}, u32[]{:S(2)}) copy-start(bf16[256,1024]{1,0:T(8,128)(2,1)} %copy-done.4) | copy-start | bytes 1572868

commit v3 on v2

--- a/solution.py
+++ b/solution.py
@@ -55,6 +55,9 @@
     me = lax.axis_index("head")
     mine = me * block_count
     distances = range(1, reach + 1)
+    relay = reach == 2 and seq_count % 2 == 0
+    odd = lax.rem(s, 2) == 1
+    relays = odd & (s >= 3)
 
     def span(h):
         return pl.ds(pl.multiple_of(h * HEAD_DIM, HEAD_DIM), HEAD_DIM)
@@ -89,13 +92,27 @@
             device_id_type=MESH,
         )
 
+    def back_target(d):
+        direct = lax.rem(s - d + seq_count, seq_count)
+        return jnp.where(odd, direct, lax.rem(s + 1, seq_count)) if relay and d == 1 else direct
+
+    def forward_copy(h, which):
+        return pltpu.make_async_remote_copy(
+            src_ref=kv_land.at[1, which, h],
+            dst_ref=kv_land.at[0, which, h],
+            send_sem=kv_send.at[0, which, h],
+            recv_sem=kv_recv.at[0, which, h],
+            device_id={"seq": lax.rem(s - 1 + seq_count, seq_count)},
+            device_id_type=MESH,
+        )
+
     def back_copy(h, d, which):
         return pltpu.make_async_remote_copy(
             src_ref=back_out.at[d - 1, which, h],
             dst_ref=back_land.at[d - 1, which, h],
             send_sem=back_send.at[d - 1, which, h],
             recv_sem=back_recv.at[d - 1, which, h],
-            device_id={"seq": lax.rem(s - d + seq_count, seq_count)},
+            device_id={"seq": back_target(d)},
             device_id_type=MESH,
         )
 
@@ -126,7 +143,16 @@
 
         each(body)
 
-    sends = lambda d: s + d < seq_count
+    def sends(d):
+        return ~odd if relay and d == 1 else s + d < seq_count
+
+    def relay_back(h):
+        for which in range(2):
+            back_copy(h, 1, which).wait_recv()
+            joined = back_out[1, which, h].astype(f32) + back_land[0, which, h].astype(f32)
+            back_out[1, which, h] = joined.astype(bf16)
+            back_copy(h, 2, which).start()
+
     takes = lambda d: s >= d
     for_pairs(sends, lambda h, d, w: kv_copy(h, d, w).start())
     for d in distances:
@@ -171,11 +197,17 @@
         adapter = dot_nn(mix_hi, lhi) + dot_nn(mix_lo, lhi) + dot_nn(mix_hi, llo)
         cot = (frozen_ref[:, span(h)].astype(f32) + adapter).astype(bf16)
         q = q_ref[:, span(h)]
-        for d in distances:
+        for d in reversed(distances):
             @pl.when(takes(d))
             def _():
                 for which in range(2):
                     kv_copy(h, d, which).wait_recv()
+
+            if relay and d == 2:
+                @pl.when(relays)
+                def _():
+                    for which in range(2):
+                        forward_copy(h, which).start()
 
         keys = [k_ref[:, span(h)]] + [kv_land[d - 1, 0, h] for d in distances]
         values = [v_ref[:, span(h)]] + [kv_land[d - 1, 1, h] for d in distances]
@@ -196,7 +228,7 @@
             back_out[d - 1, 0, h] = (dot_tn(dscore[d], q) * score_scale).astype(bf16)
             back_out[d - 1, 1, h] = dot_tn(low[d], cot).astype(bf16)
 
-            @pl.when(takes(d))
+            @pl.when(takes(d) & ~odd if relay and d == 2 else takes(d))
             def _():
                 for which in range(2):
                     back_copy(h, d, which).start()
@@ -209,7 +241,17 @@
         proj_ref[mine + block] += proj
         left_ref[:, part_span] += dot_tn(mix_hi, out) + dot_tn(mix_lo, out)
 
+        if relay:
+            @pl.when(relays & (h >= 2))
+            def _():
+                relay_back(jnp.maximum(h - 2, 0))
+
     each(one_head)
+    if relay:
+        @pl.when(relays)
+        def _():
+            for h in range(max(0, heads - 2), heads):
+                relay_back(h)
 
     for step in range(1, head_count):
         pair_copy(proj_ref, 1, step).start()
@@ -242,6 +284,10 @@
     each(finish)
     for_pairs(sends, lambda h, d, w: kv_copy(h, d, w).wait_send())
     for_pairs(takes, lambda h, d, w: back_copy(h, d, w).wait_send())
+    if relay:
+        @pl.when(relays)
+        def _():
+            each(lambda h: [forward_copy(h, w).wait_send() for w in range(2)])
 
 
 def main_call(seq_count, head_count, reach, operands):

time: 83.4 us -> 93.8 us (1.12)
  Pallas kernels: 67.3 us -> 77.7 us
    pallas_call x1, Pallas kernels: 57 us -> 65.9 us  [main_call(): pl.pallas_call(functools.partial(main_kernel, reach, seq_count, head_coun...]
    pallas_call x1, Pallas kernels: 10.4 us -> 11.8 us  [exchange_sum(): pl.pallas_call(functools.partial(exchange_kernel, seq_count, head_count),...]
where the time goes in v3:
time: 93.8 us; the launch traced here: 93.4 us
  Pallas kernels  77.7 us (83%)
  local copies, waits for them, and re-layouts  12.5 us (13%)
  other arithmetic  2.32 us (2%)
    pallas_call x1, Pallas kernels, main_call(): pl.pallas_call(functools.partial(main_kernel, reach, seq_count, head_coun...  65.9 us
    pallas_call x1, Pallas kernels, exchange_sum(): pl.pallas_call(functools.partial(exchange_kernel, seq_count, head_count),...  11.8 us
    unnamed x31, local copies, waits for them, and re-layouts  6.51 us

profile of v3, /device:TPU:0, one launch (start us, length us, event | category | flops | bytes accessed | tf_op | source)
XLA Modules:
  0.0 93.4 jit_solution(15009782605239644365)
XLA Ops:
  0.6 0.8 pad_dynamic-slice_fusion
  1.4 0.7 select_reduce_fusion.1
  2.2 0.0 copy-start.10
  2.2 0.1 copy.26.refs_6_
  2.3 0.0 copy-start.11
  2.3 1.0 %reshape.70 = f32[32,1344]{1,0:T(8,128)S(1)} reshape(f32[8,4,1344]{2,1,0:T(4,128)} %param.21) | data formatting | bytes 344064 | tf_op jit(solution)/shard_map/reshape | solution.py:416
  3.3 0.0 copy-start
  3.3 0.0 copy-start.1
  3.4 0.0 copy-start.2
  3.4 0.0 copy-start.3
  3.4 0.1 reduce-precision_convert_fusion
  3.5 0.1 pad_maximum_fusion.refs_5_
  3.6 0.0 copy-done.10
  3.6 0.0 copy-done.11
  3.6 0.2 copy.25
  3.8 0.1 reshape.71.refs_8_
  3.9 0.5 copy-done
  4.4 0.2 copy-done.1
  4.5 0.2 copy-done.2
  4.7 0.2 copy-done.3
  4.9 65.9 %shard_map.154 = (bf16[256,1024]{1,0:T(8,128)(2,1)S(1)}, bf16[256,1024]{1,0:T(8,128)(2,1)S(1)}, bf16[256,1024]{1,0:T(8,128)(2,1)S(1)}, f32[32,512]{1,0:T(8,128)S...) custom-call(bf16[256,1024]{1,0:T(8,128)(2,1)S(1)} %copy-done, bf16[256,1024]{1,0:T(8,128)(2,1)S(1)} %copy-done.1, ...), custom_call_target="tpu_custom_call" | custom-call | tf_op jit(solution)/shard_map/pallas_call | solution.py:303
  70.8 0.0 copy-start.4
  70.8 0.8 copy-done.4
  71.6 0.0 copy-start.6
  71.6 0.8 copy-done.6
  72.4 0.0 copy-start.8
  72.4 0.8 copy-done.8
  73.2 0.0 copy-start.9
  73.2 0.6 copy-done.9
  73.9 0.1 copy.27
  74.0 0.0 copy-start.12
  74.0 0.1 reshape.74
  74.1 1.1 %slice_add_fusion = f32[1,32,1344]{2,1,0:T(8,128)S(1)} fusion(f32[2,32,2688]{2,1,0:T(8,128)} %copy-done.8), kind=kLoop, calls=%fused_computation.10 | loop fusion | flops 43008 | bytes 516096 | tf_op jit(solution)/shard_map/add | solution.py:444
  75.2 0.1 add.23
  75.3 0.9 reshape.73
  76.2 0.0 copy-start.7
  76.3 0.0 copy-start.5
  76.3 0.1 copy.28
  76.3 0.0 copy-done.12
  76.4 0.2 select_reduce_fusion
  76.6 11.8 %shard_map.155 = f32[32,128]{1,0:T(8,128)S(1)} custom-call(f32[16,32,128]{2,1,0:T(8,128)S(1)} %bitcast.11), custom_call_target="tpu_custom_call" | custom-call | flops 65536 | bytes 524288 | tf_op jit(solution)/shard_map/pallas_call | solution.py:370
  88.4 0.7 slice.26
  89.1 0.6 slice.30
  89.7 0.7 reshape.77
  90.4 0.6 reshape.76
  91.0 0.0 copy-done.7
  91.0 0.8 copy.33
  91.8 0.0 copy-done.5
  91.8 0.8 copy.34
  92.6 0.8 copy.35
  (12 shorter events, 0.1 us)
Async XLA Ops:
  2.2 1.4 %copy-start.10 = (f32[8,4,512]{2,1,0:T(4,128)S(1)}, f32[8,4,512]{2,1,0:T(4,128)}, u32[]{:S(2)}) copy-start(f32[8,4,512]{2,1,0:T(4,128)} %param.20) | copy-start | bytes 196612
  2.3 1.3 %copy-start.11 = (f32[8,4,4,4]{0,3,2,1:T(4,128)S(1)}, f32[8,4,4,4]{0,3,2,1:T(4,128)}, u32[]{:S(2)}) copy-start(f32[8,4,4,4]{0,3,2,1:T(4,128)} %param.19) | copy-start | bytes 6148
  3.3 1.0 %copy-start = (bf16[256,1024]{1,0:T(8,128)(2,1)S(1)}, bf16[256,1024]{1,0:T(8,128)(2,1)}, u32[]{:S(2)}) copy-start(bf16[256,1024]{1,0:T(8,128)(2,1)} %refs_0_.1) | copy-start | bytes 1572868
  3.3 1.2 %copy-start.1 = (bf16[256,1024]{1,0:T(8,128)(2,1)S(1)}, bf16[256,1024]{1,0:T(8,128)(2,1)}, u32[]{:S(2)}) copy-start(bf16[256,1024]{1,0:T(8,128)(2,1)} %refs_1_.1) | copy-start | bytes 1572868
  3.4 1.3 %copy-start.2 = (bf16[256,1024]{1,0:T(8,128)(2,1)S(1)}, bf16[256,1024]{1,0:T(8,128)(2,1)}, u32[]{:S(2)}) copy-start(bf16[256,1024]{1,0:T(8,128)(2,1)} %refs_2_.1) | copy-start | bytes 1572868
  3.4 1.5 %copy-start.3 = (bf16[256,1024]{1,0:T(8,128)(2,1)S(1)}, bf16[256,1024]{1,0:T(8,128)(2,1)}, u32[]{:S(2)}) copy-start(bf16[256,1024]{1,0:T(8,128)(2,1)} %refs_3_.1) | copy-start | bytes 1572868
  70.8 0.8 copy-start.4
  71.6 0.8 copy-start.6
  72.4 0.8 copy-start.8
  73.2 0.6 copy-start.9
  74.0 2.4 %copy-start.12 = (s32[8]{0:T(128)S(1)}, s32[8]{0:T(128)}, u32[]{:S(2)}) copy-start(s32[8]{0:T(128)} %param.18) | copy-start | bytes 100
  76.2 14.8 %copy-start.7 = (bf16[256,1024]{1,0:T(8,128)(2,1)S(1)}, bf16[256,1024]{1,0:T(8,128)(2,1)}, u32[]{:S(2)}) copy-start(bf16[256,1024]{1,0:T(8,128)(2,1)} %copy-done.6) | copy-start | bytes 1572868
  76.3 15.5 %copy-start.5 = (bf16[256,1024]{1,0:T(8,128)(2,1)S(1)}, bf16[256,1024]{1,0:T(8,128)(2,1)}, u32[]{:S(2)}) copy-start(bf16[256,1024]{1,0:T(8,128)(2,1)} %copy-done.4) | copy-start | bytes 1572868

commit v4 on v2

--- a/solution.py
+++ b/solution.py
@@ -118,7 +118,7 @@
 
     def for_pairs(condition, act):
         def body(h):
-            for d in distances:
+            for d in reversed(distances):
                 @pl.when(condition(d))
                 def _():
                     for which in range(2):

time: 83.4 us -> 86.1 us (1.032)
  Pallas kernels: 67.3 us -> 70.1 us
    pallas_call x1, Pallas kernels: 57 us -> 59.7 us  [main_call(): pl.pallas_call(functools.partial(main_kernel, reach, seq_count, head_coun...]
where the time goes in v4:
time: 86.1 us; the launch traced here: 85.7 us
  Pallas kernels  70.1 us (81%)
  local copies, waits for them, and re-layouts  12.5 us (15%)
  other arithmetic  2.32 us (3%)
  between operations  0.89 us (1%)
    pallas_call x1, Pallas kernels, main_call(): pl.pallas_call(functools.partial(main_kernel, reach, seq_count, head_coun...  59.7 us
    pallas_call x1, Pallas kernels, exchange_sum(): pl.pallas_call(functools.partial(exchange_kernel, seq_count, head_count),...  10.4 us
    unnamed x31, local copies, waits for them, and re-layouts  6.51 us

profile of v4, /device:TPU:0, one launch (start us, length us, event | category | flops | bytes accessed | tf_op | source)
XLA Modules:
  0.0 85.7 jit_solution(8246373003436363620)
XLA Ops:
  0.6 0.8 pad_dynamic-slice_fusion
  1.4 0.7 select_reduce_fusion.1
  2.2 0.0 copy-start.10
  2.2 0.1 copy.26.refs_6_
  2.3 0.0 copy-start.11
  2.3 1.0 %reshape.70 = f32[32,1344]{1,0:T(8,128)S(1)} reshape(f32[8,4,1344]{2,1,0:T(4,128)} %param.21) | data formatting | bytes 344064 | tf_op jit(solution)/shard_map/reshape | solution.py:370
  3.3 0.0 copy-start
  3.3 0.0 copy-start.1
  3.4 0.0 copy-start.2
  3.4 0.0 copy-start.3
  3.4 0.1 reduce-precision_convert_fusion
  3.5 0.1 pad_maximum_fusion.refs_5_
  3.6 0.0 copy-done.10
  3.6 0.0 copy-done.11
  3.6 0.2 copy.25
  3.8 0.1 reshape.71.refs_8_
  3.9 0.5 copy-done
  4.4 0.2 copy-done.1
  4.5 0.2 copy-done.2
  4.7 0.2 copy-done.3
  4.9 59.7 %shard_map.154 = (bf16[256,1024]{1,0:T(8,128)(2,1)S(1)}, bf16[256,1024]{1,0:T(8,128)(2,1)S(1)}, bf16[256,1024]{1,0:T(8,128)(2,1)S(1)}, f32[32,512]{1,0:T(8,128)S...) custom-call(bf16[256,1024]{1,0:T(8,128)(2,1)S(1)} %copy-done, bf16[256,1024]{1,0:T(8,128)(2,1)S(1)} %copy-done.1, ...), custom_call_target="tpu_custom_call" | custom-call | tf_op jit(solution)/shard_map/pallas_call | solution.py:257
  64.6 0.0 copy-start.4
  64.6 0.8 copy-done.4
  65.4 0.0 copy-start.6
  65.4 0.8 copy-done.6
  66.1 0.0 copy-start.8
  66.2 0.8 copy-done.8
  67.0 0.0 copy-start.9
  67.0 0.6 copy-done.9
  67.6 0.1 copy.27
  67.7 0.0 copy-start.12
  67.8 0.1 reshape.74
  67.9 1.1 %slice_add_fusion = f32[1,32,1344]{2,1,0:T(8,128)S(1)} fusion(f32[2,32,2688]{2,1,0:T(8,128)} %copy-done.8), kind=kLoop, calls=%fused_computation.10 | loop fusion | flops 43008 | bytes 516096 | tf_op jit(solution)/shard_map/add | solution.py:398
  69.0 0.1 add.23
  69.1 0.9 %reshape.73 = f32[16,1024]{1,0:T(8,128)S(1)} reshape(f32[32,512]{1,0:T(8,128)} %copy-done.9) | data formatting | bytes 131072 | tf_op jit(solution)/shard_map/reshape | solution.py:410
  70.0 0.0 copy-start.7
  70.0 0.0 copy-start.5
  70.1 0.1 copy.28
  70.1 0.0 copy-done.12
  70.1 0.2 select_reduce_fusion
  70.4 10.4 %shard_map.155 = f32[32,128]{1,0:T(8,128)S(1)} custom-call(f32[16,32,128]{2,1,0:T(8,128)S(1)} %bitcast.11), custom_call_target="tpu_custom_call" | custom-call | flops 65536 | bytes 524288 | tf_op jit(solution)/shard_map/pallas_call | solution.py:324
  80.8 0.7 slice.26
  81.5 0.6 slice.30
  82.0 0.7 reshape.77
  82.7 0.6 reshape.76
  83.3 0.0 copy-done.7
  83.3 0.8 copy.33
  84.1 0.0 copy-done.5
  84.1 0.8 copy.34
  84.9 0.8 copy.35
  (12 shorter events, 0.1 us)
Async XLA Ops:
  2.2 1.4 %copy-start.10 = (f32[8,4,512]{2,1,0:T(4,128)S(1)}, f32[8,4,512]{2,1,0:T(4,128)}, u32[]{:S(2)}) copy-start(f32[8,4,512]{2,1,0:T(4,128)} %param.20) | copy-start | bytes 196612
  2.3 1.3 %copy-start.11 = (f32[8,4,4,4]{0,3,2,1:T(4,128)S(1)}, f32[8,4,4,4]{0,3,2,1:T(4,128)}, u32[]{:S(2)}) copy-start(f32[8,4,4,4]{0,3,2,1:T(4,128)} %param.19) | copy-start | bytes 6148
  3.3 1.0 %copy-start = (bf16[256,1024]{1,0:T(8,128)(2,1)S(1)}, bf16[256,1024]{1,0:T(8,128)(2,1)}, u32[]{:S(2)}) copy-start(bf16[256,1024]{1,0:T(8,128)(2,1)} %refs_0_.1) | copy-start | bytes 1572868
  3.3 1.2 %copy-start.1 = (bf16[256,1024]{1,0:T(8,128)(2,1)S(1)}, bf16[256,1024]{1,0:T(8,128)(2,1)}, u32[]{:S(2)}) copy-start(bf16[256,1024]{1,0:T(8,128)(2,1)} %refs_1_.1) | copy-start | bytes 1572868
  3.4 1.3 %copy-start.2 = (bf16[256,1024]{1,0:T(8,128)(2,1)S(1)}, bf16[256,1024]{1,0:T(8,128)(2,1)}, u32[]{:S(2)}) copy-start(bf16[256,1024]{1,0:T(8,128)(2,1)} %refs_2_.1) | copy-start | bytes 1572868
  3.4 1.5 %copy-start.3 = (bf16[256,1024]{1,0:T(8,128)(2,1)S(1)}, bf16[256,1024]{1,0:T(8,128)(2,1)}, u32[]{:S(2)}) copy-start(bf16[256,1024]{1,0:T(8,128)(2,1)} %refs_3_.1) | copy-start | bytes 1572868
  64.6 0.8 copy-start.4
  65.4 0.8 copy-start.6
  66.1 0.8 copy-start.8
  67.0 0.6 copy-start.9
  67.7 2.4 %copy-start.12 = (s32[8]{0:T(128)S(1)}, s32[8]{0:T(128)}, u32[]{:S(2)}) copy-start(s32[8]{0:T(128)} %param.18) | copy-start | bytes 100
  70.0 13.4 %copy-start.7 = (bf16[256,1024]{1,0:T(8,128)(2,1)S(1)}, bf16[256,1024]{1,0:T(8,128)(2,1)}, u32[]{:S(2)}) copy-start(bf16[256,1024]{1,0:T(8,128)(2,1)} %copy-done.6) | copy-start | bytes 1572868
  70.0 14.1 %copy-start.5 = (bf16[256,1024]{1,0:T(8,128)(2,1)S(1)}, bf16[256,1024]{1,0:T(8,128)(2,1)}, u32[]{:S(2)}) copy-start(bf16[256,1024]{1,0:T(8,128)(2,1)} %copy-done.4) | copy-start | bytes 1572868
